TPU v7x, 128 devices: a whole 4x4x4 slice. The times are simulated.
128 devices in a mesh: gx: 16 (over z, x), gy: 8 (over y, core).
Axes of the slice: x: 4, y: 4, z: 4, core: 2. Of those that a mesh axis runs over, the one named last changes fastest.
Arguments:
- grid_now: float32 [3, 256, 256, 512], P(None, 'gx', 'gy'), may hold values from -6 to 6
- grid_before: float32 [3, 256, 256, 512], P(None, 'gx', 'gy'), may hold values from -6 to 6
- wave_factor: float32 [256, 256, 512], P('gx', 'gy'), may hold values from 0.04 to 0.2
- layer_owner: int32 [16, 4096, 1], P('gx', 'gy'), may hold values from 0 to 127; in each aligned block of 512 rows (0 to 511, 512 to 1023, ..., all dimensions but the last counted through in order) at most 8 rows name the same one
- layer_cell: int32 [16, 4096], P('gx', 'gy'), may hold values from 0 to 262143
- box_now: float32 [3, 16, 71680], P(None, 'gx', 'gy'), may hold values from -6 to 6
- box_before: float32 [3, 16, 71680], P(None, 'gx', 'gy'), may hold values from -6 to 6
- node_mass: float32 [16, 71680], P('gx', 'gy'), may hold values from 0.5 to 2
- corner_nodes: int32 [8, 16, 65536], P(None, 'gx', 'gy'), may hold values from 0 to 71679, as said below
- live_counts: int32 [16, 8], P('gx', 'gy'), may hold values from 2048 to 8192, as said below
- shear_modulus: float32 [16, 65536], P('gx', 'gy'), may hold values from 0.25 to 2
- lame_lambda: float32 [16, 65536], P('gx', 'gy'), may hold values from 0.5 to 4
- strain_scale: float32 [16, 65536], P('gx', 'gy'), may hold values from 0.2 to 2
- layer_nodes: int32 [16, 4096], P('gx', 'gy'), may hold values from 0 to 71679, as said below
Outputs:
- grid_after: float32 [3, 256, 256, 512], P(None, 'gx', 'gy')
- box_after: float32 [3, 16, 71680], P(None, 'gx', 'gy')
Inputs may be any that keep to these rules, and one draw needn't show every extreme that they name: `layer_owner`: owners are numbered gx index times 8 plus gy index; among the 512 layer slots of one device at most 8 name the same owner. `layer_cell`: cells are numbered (x * 32 + y) * 512 + z within the owner's block. `corner_nodes`: corner a of an element sits at offsets (a % 2, a // 2 % 2, a // 4) of a unit cube; for each corner a, distinct element slots of a box name distinct nodes. `live_counts`: live slots come first in each device's block of 8192 slots. `layer_nodes`: the layer nodes of one box are distinct.
All inputs are finite; a program needn't handle non-finite values.
Results may differ from a plain program's by a relative error of at most 0.0003.
Values sent between devices are 32-bit elements; how exact they have to be, the bound alone decides.
A program may use at most 384 MiB of HBM per device.

v0:
```python
import jax
import jax.numpy as jnp
from jax import lax
from jax.sharding import PartitionSpec as P

PENALTY = 2.0
STEP_SQUARE = 0.25


def extended_2(block, sides, width):
    for axis, dim in sides:
        count = lax.axis_size(axis)
        forward = [(i, i + 1) for i in range(count - 1)]
        backward = [(target, source) for source, target in forward]
        low = lax.ppermute(
            lax.slice_in_dim(block, block.shape[dim] - width, None, axis=dim), axis, forward
        )
        high = lax.ppermute(lax.slice_in_dim(block, 0, width, axis=dim), axis, backward)
        block = jnp.concatenate([low, block, high], axis=dim)
    return block


def stencil(extended, row_count, col_count):
    padded = jnp.pad(extended, ((0, 0), (0, 0), (0, 0), (2, 2)))
    channels = extended.shape[0]
    extent = extended.shape[3]

    def shifted(along_x, along_y, along_z):
        return lax.slice(
            padded,
            (0, 2 + along_x, 2 + along_y, 2 + along_z),
            (channels, 2 + along_x + row_count, 2 + along_y + col_count, 2 + along_z + extent),
        )

    result = -7.5 * shifted(0, 0, 0)
    for offset, weight in ((1, 16.0 / 12.0), (2, -1.0 / 12.0)):
        for orient in (1, -1):
            result = result + weight * (
                shifted(orient * offset, 0, 0)
                + shifted(0, orient * offset, 0)
                + shifted(0, 0, orient * offset)
            )
    return result


def corner_gradients():
    corner = jnp.arange(8)
    bit_rows = jnp.stack([corner // 2**level % 2 for level in range(3)])
    return (2.0 * bit_rows.astype(jnp.float32) - 1.0) * 0.25


def element_forces(corner_disp, shear, lame, scale, weights):
    gradients = corner_gradients()
    disp_grad = jnp.einsum("ja,iae->ije", gradients, corner_disp, precision=lax.Precision.HIGHEST)
    strain = 0.5 * (disp_grad + jnp.transpose(disp_grad, (1, 0, 2)))
    trace = strain[0, 0] + strain[1, 1] + strain[2, 2]
    identity = jnp.eye(3, dtype=jnp.float32)[:, :, None]
    deviator = strain - identity * (trace / 3.0)
    invariant = jnp.sum(deviator * deviator, axis=(0, 1))
    softened = shear / (1.0 + invariant / scale)
    stress = (identity * (lame * trace) + 2.0 * softened * strain) * weights
    return jnp.einsum("ja,ije->iae", gradients, stress, precision=lax.Precision.HIGHEST)


def advance(current, previous, factor):
    extended = extended_2(current, (("gx", 1), ("gy", 2)), 2)
    return 2.0 * current - previous + factor * stencil(extended, current.shape[1], current.shape[2])


def on_device(
    grid_now,
    grid_before,
    wave_factor,
    layer_owner,
    layer_cell,
    box_now,
    box_before,
    node_mass,
    corner_nodes,
    live_counts,
    shear_modulus,
    lame_lambda,
    strain_scale,
    layer_nodes,
):
    factor = wave_factor[None]
    grid_mid = advance(grid_now, grid_before, factor)
    grid_after = advance(grid_mid, grid_now, factor)
    owners = layer_owner.reshape(-1)
    cell_index = layer_cell.reshape(-1)
    count_gx = lax.axis_size("gx")
    count_gy = lax.axis_size("gy")
    devices = count_gx * count_gy
    capacity = 2 * owners.shape[0] // devices
    rank_rows = jnp.arange(owners.shape[0])
    earlier = (rank_rows[None, :] < rank_rows[:, None]).astype(jnp.bfloat16)
    matches = owners[:, None] == jnp.arange(devices)[None, :]
    before = jnp.dot(earlier, matches.astype(jnp.bfloat16), preferred_element_type=jnp.float32)
    position = jnp.sum(jnp.where(matches, before, 0.0), axis=1).astype(jnp.int32)
    slot_index = owners * capacity + position
    requests = (
        jnp.zeros((devices * capacity,), jnp.int32)
        .at[slot_index]
        .set(cell_index, unique_indices=True)
    )
    flat_field = grid_after.reshape(3, -1)
    wanted = lax.all_to_all(
        requests.reshape(devices, capacity), ("gx", "gy"), split_axis=0, concat_axis=0, tiled=True
    )
    gathered = jnp.take(flat_field, wanted.reshape(-1), axis=1, mode="clip").reshape(
        3, wanted.shape[0], wanted.shape[1]
    )
    returned = lax.all_to_all(gathered, ("gx", "gy"), split_axis=1, concat_axis=1, tiled=True)
    replies = returned.reshape(3, devices * capacity)
    motion = jnp.take(replies, slot_index, axis=1, mode="clip")
    own_disp = box_now.reshape(3, -1)
    all_disp = lax.all_gather(own_disp, "gy", axis=1, tiled=True)
    corner_ids = corner_nodes.reshape(8, -1)
    live_count = live_counts.reshape(())
    weights = (jnp.arange(corner_ids.shape[1]) < live_count).astype(jnp.float32)
    corner_disp = jnp.take(all_disp, corner_ids.reshape(-1), axis=1, mode="clip").reshape(3, 8, -1)
    forces = element_forces(
        corner_disp,
        shear_modulus.reshape(-1),
        lame_lambda.reshape(-1),
        strain_scale.reshape(-1),
        weights,
    )
    node_term = jnp.zeros_like(all_disp)
    for corner in range(8):
        node_term = node_term.at[:, corner_ids[corner]].add(-forces[:, corner], unique_indices=True)
    layer_ids = layer_nodes.reshape(-1)
    node_term = node_term.at[:, layer_ids].add(
        PENALTY * (motion - jnp.take(all_disp, layer_ids, axis=1, mode="clip")), unique_indices=True
    )
    summed = lax.psum_scatter(node_term, "gy", scatter_dimension=1, tiled=True)
    box_after = 2.0 * own_disp - box_before.reshape(3, -1) + STEP_SQUARE / node_mass * summed
    return (grid_after, box_after.reshape(box_now.shape))


def solution(mesh):
    return jax.shard_map(
        on_device,
        mesh=mesh,
        in_specs=(
            P(None, "gx", "gy", None),
            P(None, "gx", "gy", None),
            P("gx", "gy", None),
            P("gx", "gy", None),
            P("gx", "gy"),
            P(None, "gx", "gy"),
            P(None, "gx", "gy"),
            P("gx", "gy"),
            P(None, "gx", "gy"),
            P("gx", "gy"),
            P("gx", "gy"),
            P("gx", "gy"),
            P("gx", "gy"),
            P("gx", "gy"),
        ),
        out_specs=(P(None, "gx", "gy", None), P(None, "gx", "gy")),
        check_vma=False,
    )
```

profile of v0, /device:TPU:4, one launch (start us, length us, event | category | flops | bytes accessed | tf_op | source)
XLA Modules:
  0.0 1384.2 jit_solution(17352762982526760469)
XLA Ops:
  7.2 1.2 fusion.67
  8.4 2.4 collective-permute-start
  10.8 3.4 collective-permute-start.1
  14.2 1.1 fusion.32
  15.3 0.7 compare_select_fusion.8
  16.0 2.6 scatter_custom_fusion.8
  18.6 0.7 all_to_all.9
  19.3 12.6 all-to-all-start
  32.0 3.6 copy.175
  35.6 155.6 %all-gather = f32[3,1,71680]{0,2,1:T(8,128)} all-gather(f32[3,1,8960]{0,2,1:T(8,128)} %copy.175), channel_id=2, replica_groups=mesh['gx'=16,'gy'=8] {'gy'}, dimensions={2}, use_global_device_ids=true | all-gather | bytes 967680 | tf_op jit(solution)/shard_map/all_gather | solution.py:117
  191.2 227.4 %gather_fusion = f32[65536,3]{1,0:T(8,128)} fusion(f32[3,71680]{0,1:T(8,128)} %bitcast.126, s32[65536]{0:T(1024)S(1)} %broadcast_clamp_fusion), kind=kCustom, calls=%fused_computation | custom fusion | bytes 1835008 | tf_op jit(solution)/shard_map/jit(_take)/gather | solution.py:121
  418.6 18.1 %copy.176 = f32[3,8,8192]{2,1,0:T(8,128)S(1)} copy(f32[3,8,8192]{0,2,1:T(8,128)} %bitcast.129) | data formatting | bytes 1572864 | tf_op jit(solution)/shard_map/reshape | solution.py:121
  436.8 0.8 fusion.50
  439.3 0.9 convolution_bitcast_fusion
  440.3 1.8 constant_dynamic-update-slice_fusion.1
  443.2 1.3 collective-permute-start.2
  444.5 3.3 collective-permute-start.3
  447.7 1.6 slice_negate_fusion
  450.0 3.8 pad_maximum_fusion
  453.8 4.6 select_maximum_fusion.4
  458.4 12.6 fusion.25
  471.6 2.5 collective-permute-start.4
  474.1 3.4 collective-permute-start.5
  477.5 1.0 compare_select_fusion
  479.1 4.5 collective-permute-done.4
  483.9 2.5 collective-permute-done.5
  486.8 0.7 copy-done.3
  487.5 1.0 pad_maximum_fusion.5
  488.4 1.3 collective-permute-start.6
  489.7 5.0 collective-permute-start.7
  494.8 0.7 divide_reduce_fusion
  496.0 2.2 reduce.5
  498.2 0.9 reshape.564
  499.2 3.4 pad_maximum_fusion.1
  502.6 5.7 select_maximum_fusion
  508.3 11.0 fusion.11
  519.3 63.8 %copy.187 = f32[3,16,32,512]{0,3,2,1:T(8,128)} copy(f32[3,16,32,512]{3,1,2,0:T(8,128)} %fusion.11) | data formatting | bytes 6291456 | tf_op jit(solution)/shard_map/add | solution.py:67
  583.0 24.1 %gather_fusion.1 = f32[1024,3]{1,0:T(8,128)S(1)} fusion(f32[3,262144]{0,1:T(8,128)} %bitcast.40, s32[1024]{0:T(1024)S(1)} %broadcast_clamp_fusion.1), kind=kCustom, calls=%fused_computation.1 | custom fusion | bytes 28672 | tf_op jit(solution)/shard_map/jit(_take)/gather | solution.py:110
  607.2 1.5 copy.189
  608.7 20.4 %all-to-all-start.1 = ((f32[3,128,8]{2,0,1:T(4,128)}), f32[3,128,8]{2,0,1:T(4,128)S(1)}, u32[]{:S(2)}, u32[]{:S(2)}) async-start(f32[3,128,8]{2,0,1:T(4,128)} %copy.189), calls=%async_computation.1 | async-start | bytes 524288 | tf_op jit(solution)/shard_map/all_to_all | solution.py:113
  629.4 2.7 copy.179
  632.2 2.7 copy.180
  634.9 2.7 copy.181
  637.7 2.6 copy.182
  640.4 2.6 copy.183
  643.1 2.7 copy.184
  645.9 2.7 copy.185
  648.6 2.6 copy.186
  651.3 58.9 %scatter_custom_fusion = f32[3,71680]{0,1:T(8,128)} fusion(s32[8192]{0:T(1024)} %bitcast.151, f32[8192,3]{1,0:T(8,128)} %copy.179, f32[]{:T(128)} %constant.85.clone.1), kind=kCustom, calls=%fused_computation.14 | custom fusion | flops 24576 | bytes 860672 | tf_op jit(solution)/shard_map/scatter-add | solution.py:131
  710.2 63.4 %scatter_fusion = f32[3,71680]{0,1:T(8,128)} fusion(f32[3,71680]{0,1:T(8,128)} %scatter_custom_fusion, s32[8192]{0:T(1024)S(1)} %bitcast.148, f32[8192,3]{1,0:T(8,128)} %copy.180), kind=kCustom, calls=%fused_computation.5 | custom fusion | flops 24576 | bytes 327680 | tf_op jit(solution)/shard_map/scatter-add | solution.py:131
  773.6 63.4 %scatter_fusion.1 = f32[3,71680]{0,1:T(8,128)} fusion(f32[3,71680]{0,1:T(8,128)} %scatter_fusion, s32[8192]{0:T(1024)S(1)} %bitcast.147, f32[8192,3]{1,0:T(8,128)} %copy.181), kind=kCustom, calls=%fused_computation.6 | custom fusion | flops 24576 | bytes 327680 | tf_op jit(solution)/shard_map/scatter-add | solution.py:131
  837.0 63.4 %scatter_fusion.2 = f32[3,71680]{0,1:T(8,128)} fusion(f32[3,71680]{0,1:T(8,128)} %scatter_fusion.1, s32[8192]{0:T(1024)S(1)} %bitcast.146, f32[8192,3]{1,0:T(8,128)} %copy.182), kind=kCustom, calls=%fused_computation.7 | custom fusion | flops 24576 | bytes 327680 | tf_op jit(solution)/shard_map/scatter-add | solution.py:131
  900.4 63.4 %scatter_fusion.3 = f32[3,71680]{0,1:T(8,128)} fusion(f32[3,71680]{0,1:T(8,128)} %scatter_fusion.2, s32[8192]{0:T(1024)S(1)} %bitcast.145, f32[8192,3]{1,0:T(8,128)} %copy.183), kind=kCustom, calls=%fused_computation.8 | custom fusion | flops 24576 | bytes 327680 | tf_op jit(solution)/shard_map/scatter-add | solution.py:131
  963.8 63.6 %scatter_fusion.4 = f32[3,71680]{0,1:T(8,128)} fusion(f32[3,71680]{0,1:T(8,128)} %scatter_fusion.3, s32[8192]{0:T(1024)S(1)} %bitcast.144, f32[8192,3]{1,0:T(8,128)} %copy.184), kind=kCustom, calls=%fused_computation.9 | custom fusion | flops 24576 | bytes 327680 | tf_op jit(solution)/shard_map/scatter-add | solution.py:131
  1027.4 63.4 %scatter_fusion.5 = f32[3,71680]{0,1:T(8,128)} fusion(f32[3,71680]{0,1:T(8,128)} %scatter_fusion.4, s32[8192]{0:T(1024)S(1)} %bitcast.143, f32[8192,3]{1,0:T(8,128)} %copy.185), kind=kCustom, calls=%fused_computation.10 | custom fusion | flops 24576 | bytes 327680 | tf_op jit(solution)/shard_map/scatter-add | solution.py:131
  1090.8 63.4 %scatter_fusion.6 = f32[3,71680]{0,1:T(8,128)} fusion(f32[3,71680]{0,1:T(8,128)} %scatter_fusion.5, s32[8192]{0:T(1024)S(1)} %bitcast.142, f32[8192,3]{1,0:T(8,128)} %copy.186), kind=kCustom, calls=%fused_computation.11 | custom fusion | flops 24576 | bytes 327680 | tf_op jit(solution)/shard_map/scatter-add | solution.py:131
  1154.2 0.8 copy.190
  1155.0 31.1 %scatter_custom_fusion.9 = f32[3,71680]{0,1:T(8,128)} fusion(f32[3,71680]{0,1:T(8,128)} %scatter_fusion.6, s32[512]{0:T(512)} %bitcast.157, f32[]{:T(128)} %constant.83.clone.1, f32[3,71680]{0,1:T(8,128)} %bitcast.127, s32[1024]{0:T(1024)S(1)} %get-tuple-element.52, f32[3,1024]{0,1:T(8,128)S(1)} %bitcast.131, s32[1024]{0:T(1024)S(1)} %get-tuple-element.53), kind=kCustom, calls=%fused_computation.95 | custom fusion | flops 4608 | bytes 37581312 | tf_op jit(solution)/shard_map/scatter-add | solution.py:133
  1186.1 0.9 copy-done.9
  1187.2 0.9 copy-done
  1188.1 3.5 copy.192
  1191.6 181.5 %reduce-scatter.4.cloned.1.call-done = f32[8960,3]{1,0:T(8,128)} async-done(((f32[71680,3]{1,0:T(8,128)}), f32[8960,3]{1,0:T(8,128)}) %reduce-scatter.4.cloned.1.call-update) | async-done | bytes 107536
  1373.1 3.0 copy.195
  1376.2 0.8 copy.193
  (106 shorter events, 6.1 us)
Async XLA Ops:
  8.4 434.1 %collective-permute-start = (f32[3,2,32,512]{3,2,1,0:T(8,128)S(1)}, f32[3,2,32,512]{3,2,1,0:T(8,128)S(1)}, u32[]{:S(2)}, u32[]{:S(2)}) collective-permute-start(f32[3,2,32,512]{3,2,1,0:T(8,128)S(1)} %get-tuple-element.30), channel_id=1, source_target_pairs={{8,0},{16,8},{24,16},{32,24},{40,32},{48,40},{56,48},{64,56},{72,6... | collective-permute-start | bytes 1179656 | tf_op jit(solution)/shard_map/ppermute | solution.py:18
  10.8 431.3 %collective-permute-start.1 = (f32[3,2,32,512]{3,2,1,0:T(8,128)S(1)}, f32[3,2,32,512]{3,2,1,0:T(8,128)S(1)}, u32[]{:S(2)}, u32[]{:S(2)}) collective-permute-start(f32[3,2,32,512]{3,2,1,0:T(8,128)S(1)} %get-tuple-element.31), channel_id=1, source_target_pairs={{0,8},{8,16},{16,24},{24,32},{32,40},{40,48},{48,56},{56,64},{64,7... | collective-permute-start | bytes 1179656 | tf_op jit(solution)/shard_map/ppermute | solution.py:15
  19.3 476.2 %all-to-all-start = ((s32[128,1,8]{2,1,0:T(1,128)}), s32[128,1,8]{2,1,0:T(1,128)}, u32[]{:S(2)}, u32[]{:S(2)}) async-start(s32[128,1,8]{2,1,0:T(1,128)} %bitcast.46), calls=%async_computation | async-start | bytes 131072 | tf_op jit(solution)/shard_map/all_to_all | solution.py:107
  35.6 155.6 %copy-start.8 = (s32[8,1,8192]{2,1,0:T(1,128)S(1)}, s32[8,1,8192]{2,1,0:T(1,128)}, u32[]{:S(2)}) copy-start(s32[8,1,8192]{2,1,0:T(1,128)} %param.22) | copy-start | bytes 786436
  418.6 19.2 %copy-start.28 = (f32[1,8192]{1,0:T(1,128)S(1)}, f32[1,8192]{1,0:T(1,128)}, u32[]{:S(2)}) copy-start(f32[1,8192]{1,0:T(1,128)} %param.25) | copy-start | bytes 98308
  418.6 20.4 %copy-start.29 = (f32[1,8192]{1,0:T(1,128)S(1)}, f32[1,8192]{1,0:T(1,128)}, u32[]{:S(2)}) copy-start(f32[1,8192]{1,0:T(1,128)} %param.24) | copy-start | bytes 98308
  418.6 20.4 %copy-start.30 = (f32[1,8192]{1,0:T(1,128)S(1)}, f32[1,8192]{1,0:T(1,128)}, u32[]{:S(2)}) copy-start(f32[1,8192]{1,0:T(1,128)} %param.26) | copy-start | bytes 98308
  436.8 3.5 copy-start.2
  442.1 7.2 copy-start.7
  443.0 6.9 copy-start.1
  443.2 6.8 collective-permute-start.2
  444.5 5.5 collective-permute-start.3
  449.9 8.5 copy-start.5
  458.4 20.1 %copy-start.31 = (s32[1,512]{1,0:T(1,128)S(1)}, s32[1,512]{1,0:T(1,128)}, u32[]{:S(2)}) copy-start(s32[1,512]{1,0:T(1,128)} %param.27) | copy-start | bytes 6148
  471.5 23.3 %copy-start.27 = (f32[1,8960]{1,0:T(1,128)S(1)}, f32[1,8960]{1,0:T(1,128)}, u32[]{:S(2)}) copy-start(f32[1,8960]{1,0:T(1,128)} %param.21) | copy-start | bytes 107524
  471.6 12.0 collective-permute-start.4
  474.1 12.3 collective-permute-start.5
  486.7 0.8 copy-start.3
  488.4 10.7 collective-permute-start.6
  489.7 9.5 collective-permute-start.7
  499.2 3.4 copy-start.4
  502.6 5.7 copy-start.6
  519.3 110.0 %copy-start.17 = (f32[3,1,8192]{2,1,0:T(1,128)S(1)}, f32[3,1,8192]{2,1,0:T(1,128)}, u32[]{:S(2)}) copy-start(f32[3,1,8192]{2,1,0:T(1,128)} %get-tuple-element.39) | copy-start | bytes 294916
  608.7 545.5 %all-to-all-start.1 = ((f32[3,128,8]{2,0,1:T(4,128)}), f32[3,128,8]{2,0,1:T(4,128)S(1)}, u32[]{:S(2)}, u32[]{:S(2)}) async-start(f32[3,128,8]{2,0,1:T(4,128)} %copy.189), calls=%async_computation.1 | async-start | bytes 524288 | tf_op jit(solution)/shard_map/all_to_all | solution.py:113
  629.1 744.0 %reduce-scatter.4.cloned.1.call-start = ((), (), s32[]{:S(2)}) async-start(), calls=%async_computation.3 | async-start | bytes 41287680
  629.4 2.7 copy-start.16
  632.2 2.7 copy-start.15
  634.9 2.7 copy-start.14
  637.7 2.7 copy-start.13
  640.4 2.6 copy-start.12
  643.1 2.7 copy-start.11
  645.9 2.7 copy-start.10
  651.3 58.9 %copy-start.25 = (s32[8192,1]{0,1:T(1,128)S(1)}, s32[8192,1]{0,1:T(1,128)}, u32[]{:S(2)}) copy-start(s32[8192,1]{0,1:T(1,128)} %get-tuple-element.47) | copy-start | bytes 98308
  651.3 122.3 %copy-start.24 = (s32[8192,1]{0,1:T(1,128)S(1)}, s32[8192,1]{0,1:T(1,128)}, u32[]{:S(2)}) copy-start(s32[8192,1]{0,1:T(1,128)} %get-tuple-element.46) | copy-start | bytes 98308
  710.2 126.8 %copy-start.23 = (s32[8192,1]{0,1:T(1,128)S(1)}, s32[8192,1]{0,1:T(1,128)}, u32[]{:S(2)}) copy-start(s32[8192,1]{0,1:T(1,128)} %get-tuple-element.45) | copy-start | bytes 98308
  710.2 190.2 %copy-start.22 = (s32[8192,1]{0,1:T(1,128)S(1)}, s32[8192,1]{0,1:T(1,128)}, u32[]{:S(2)}) copy-start(s32[8192,1]{0,1:T(1,128)} %get-tuple-element.44) | copy-start | bytes 98308
  710.2 253.6 %copy-start.21 = (s32[8192,1]{0,1:T(1,128)S(1)}, s32[8192,1]{0,1:T(1,128)}, u32[]{:S(2)}) copy-start(s32[8192,1]{0,1:T(1,128)} %get-tuple-element.43) | copy-start | bytes 98308
  773.6 253.8 %copy-start.20 = (s32[8192,1]{0,1:T(1,128)S(1)}, s32[8192,1]{0,1:T(1,128)}, u32[]{:S(2)}) copy-start(s32[8192,1]{0,1:T(1,128)} %get-tuple-element.49) | copy-start | bytes 98308
  837.0 253.8 %copy-start.19 = (s32[8192,1]{0,1:T(1,128)S(1)}, s32[8192,1]{0,1:T(1,128)}, u32[]{:S(2)}) copy-start(s32[8192,1]{0,1:T(1,128)} %get-tuple-element.42) | copy-start | bytes 98308
  1186.1 0.9 copy-start.9
  1186.1 0.9 copy-start.26
  1186.1 2.0 copy-start
  1188.1 188.0 %copy-start.18 = (f32[8960]{0:T(1024)S(1)}, f32[8960]{0:T(1024)}, u32[]{:S(2)}) copy-start(f32[8960]{0:T(1024)} %divide_reduce_fusion) | copy-start | bytes 107524
Sparse Core Ops, SparseCore 0:
  1186.2 186.7 reduce-scatter.3
where the time goes:
time: 1390 us; the launch traced here: 1380 us
  other arithmetic  584 us (42%)
  local copies, waits for them, and re-layouts  382 us (27%)
  waiting for transfers between devices  189 us (14%)
  blocking collectives  156 us (11%)
  starting transfers between devices  55.8 us (4%)
  between operations  15.8 us (1%)
    scatter-add x8, other arithmetic, on_device(): node_term.at[:, corner_ids[corner]]  503 us
    gather x1, local copies, waits for them, and re-layouts, on_device(): jnp.take(all_disp, corner_ids.reshape(-1), axis=1, mode='clip')  227 us
    unnamed x2, waiting for transfers between devices  181 us
    all_gather x1, blocking collectives, on_device(): all_disp = lax.all_gather(own_disp, 'gy', axis=1, tiled=True)  156 us
    add x1, local copies, waits for them, and re-layouts, advance(): 2.0 * current - previous  63.8 us
    scatter-add x1, other arithmetic, on_device(): node_term.at[:, layer_ids]  31.1 us
  transfers between devices with their start and end apart: 11, of which 3 were waited for; matrix products, arithmetic and copies ran while one was open for 59% of the time, Pallas kernels for 0%

commit v1 on v0

v1 whole, which is shorter than its diff:
```python
import functools

import jax
import jax.numpy as jnp
from jax import lax
from jax.experimental import pallas as pl
from jax.experimental.pallas import tpu as pltpu
from jax.sharding import PartitionSpec as P

PENALTY = 2.0
STEP_SQUARE = 0.25
LANES = 128
SLOTS = 16
VMEM_LIMIT = 56 * 2**20
GATHER_UNROLL = 8
SCATTER_UNROLL = 16
LAYER_UNROLL = 16


def gradient_signs(corner):
    lane = lax.broadcasted_iota(jnp.int32, (1, LANES), 1)
    signs = jnp.zeros((1, LANES), jnp.float32)
    for direction in range(3):
        value = 0.25 if (corner >> direction) & 1 else -0.25
        inside = (lane >= 3 * direction) & (lane < 3 * direction + 3)
        signs = jnp.where(inside, value, signs)
    return signs


def rows_of(values):
    count = values.shape[0]
    padded = jnp.concatenate(
        [values, jnp.zeros((SLOTS - count, LANES), jnp.float32)], axis=0
    )
    return padded.T


def aligned(start):
    return pl.multiple_of(start, LANES)


def gather_kernel(
    live_ref, layer_ref, corner_hbm, disp_ref, shear_ref, lame_ref, scale_ref,
    stress_ref, layer_out, table, grad_rows, layer_rows, *rest,
):
    ids, sems = rest[:8], rest[8]
    copies = [
        pltpu.make_async_copy(corner_hbm.at[corner, 0], ids[corner], sems.at[corner])
        for corner in range(8)
    ]
    for copy in copies:
        copy.start()
    owners, _, own = disp_ref.shape

    def build(part, carry):
        for tile in range(own // LANES):
            block = disp_ref[part, :, tile * LANES : (tile + 1) * LANES]
            rows = rows_of(jnp.concatenate([block, block, block], axis=0))
            table[pl.ds(aligned(part * own + tile * LANES), LANES), 0:SLOTS] = rows
        return carry

    lax.fori_loop(0, owners, build, 0)
    for copy in copies:
        copy.wait()
    signs = [gradient_signs(corner) for corner in range(4)]
    live = live_ref[0, 0]

    def gather(chunk, carry):
        base = chunk * GATHER_UNROLL
        for step in range(GATHER_UNROLL):
            slot = base + step
            rows = [table[pl.ds(ids[corner][slot], 1), :] for corner in range(8)]
            spans = [rows[corner] - rows[7 - corner] for corner in range(4)]
            grad_rows[pl.ds(slot, 1), :] = (spans[0] * signs[0] + spans[1] * signs[1]) + (
                spans[2] * signs[2] + spans[3] * signs[3]
            )
        return carry

    lax.fori_loop(0, (live + GATHER_UNROLL - 1) // GATHER_UNROLL, gather, 0)

    def layer(chunk, carry):
        base = chunk * LAYER_UNROLL
        for step in range(LAYER_UNROLL):
            node = layer_ref[0, base + step]
            layer_rows[pl.ds(base + step, 1), :] = table[pl.ds(node, 1), :]
        return carry

    lax.fori_loop(0, layer_rows.shape[0] // LAYER_UNROLL, layer, 0)
    for tile in range(layer_rows.shape[0] // LANES):
        block = layer_rows[tile * LANES : (tile + 1) * LANES, 0:SLOTS].T
        layer_out[:, tile * LANES : (tile + 1) * LANES] = block[0:3] * -PENALTY

    def element(tile, carry):
        start = aligned(tile * LANES)
        grads = grad_rows[pl.ds(start, LANES), 0:SLOTS].T
        slope = [[grads[3 * j + i : 3 * j + i + 1] for j in range(3)] for i in range(3)]
        s00, s11, s22 = slope[0][0], slope[1][1], slope[2][2]
        s01 = 0.5 * (slope[0][1] + slope[1][0])
        s02 = 0.5 * (slope[0][2] + slope[2][0])
        s12 = 0.5 * (slope[1][2] + slope[2][1])
        trace = s00 + s11 + s22
        mean = trace / 3.0
        d00, d11, d22 = s00 - mean, s11 - mean, s22 - mean
        invariant = d00 * d00 + d11 * d11 + d22 * d22
        invariant = invariant + 2.0 * (s01 * s01 + s02 * s02 + s12 * s12)
        here = pl.ds(start, LANES)
        softened = 2.0 * shear_ref[:, here] / (1.0 + invariant / scale_ref[:, here])
        volume = lame_ref[:, here] * trace
        index = start + lax.broadcasted_iota(jnp.int32, (1, LANES), 1)

        def signed(value):
            return jnp.where(index < live, -value, 0.0)

        p00 = signed(volume + softened * s00)
        p11 = signed(volume + softened * s11)
        p22 = signed(volume + softened * s22)
        p01, p02, p12 = signed(softened * s01), signed(softened * s02), signed(softened * s12)
        stress_ref[tile] = jnp.concatenate(
            [p00, p01, p02, p01, p11, p12, p02, p12, p22, jnp.zeros((7, LANES), jnp.float32)],
            axis=0,
        )
        return carry

    lax.fori_loop(0, stress_ref.shape[0], element, 0)


def scatter_kernel(
    live_ref, layer_ref, slot_ref, corner_hbm, stress_ref, layer_in, reply_ref,
    out_ref, total, stress_rows, layer_rows, reply_rows, *rest,
):
    ids, sems = rest[:8], rest[8]
    copies = [
        pltpu.make_async_copy(corner_hbm.at[corner, 0], ids[corner], sems.at[corner])
        for corner in range(8)
    ]
    for copy in copies:
        copy.start()
    owners, _, own = out_ref.shape

    def clear(chunk, carry):
        zero = jnp.zeros((LANES, LANES), jnp.float32)
        total[pl.ds(aligned(chunk * LANES), LANES), :] = zero
        return carry

    lax.fori_loop(0, total.shape[0] // LANES, clear, 0)

    def to_rows(tile, carry):
        stress_rows[pl.ds(aligned(tile * LANES), LANES), 0:SLOTS] = stress_ref[tile].T
        return carry

    lax.fori_loop(0, stress_ref.shape[0], to_rows, 0)
    for tile in range(layer_rows.shape[0] // LANES):
        here = slice(tile * LANES, (tile + 1) * LANES)
        layer_rows[here, 0:SLOTS] = rows_of(layer_in[:, here])
    for tile in range(reply_rows.shape[0] // LANES):
        here = slice(tile * LANES, (tile + 1) * LANES)
        reply_rows[here, 0:SLOTS] = rows_of(reply_ref[:, here] * PENALTY)
    for copy in copies:
        copy.wait()
    signs = [gradient_signs(corner) for corner in range(8)]
    live = live_ref[0, 0]

    def scatter(chunk, carry):
        base = chunk * SCATTER_UNROLL
        steps = range(SCATTER_UNROLL)
        rows = [stress_rows[pl.ds(base + step, 1), :] for step in steps]
        for corner in range(8):
            nodes = [ids[corner][base + step] for step in steps]
            held = [total[pl.ds(nodes[step], 1), :] for step in steps]
            held = [held[step] + rows[step] * signs[corner] for step in steps]
            for step in steps:
                total[pl.ds(nodes[step], 1), :] = held[step]
        return carry

    lax.fori_loop(0, (live + SCATTER_UNROLL - 1) // SCATTER_UNROLL, scatter, 0)

    def layer(chunk, carry):
        base = chunk * LAYER_UNROLL
        steps = range(LAYER_UNROLL)
        nodes = [layer_ref[0, base + step] for step in steps]
        held = [total[pl.ds(nodes[step], 1), :] for step in steps]
        for step in steps:
            reply = reply_rows[pl.ds(slot_ref[0, base + step], 1), :]
            held[step] = held[step] + (reply + layer_rows[pl.ds(base + step, 1), :])
        for step in steps:
            total[pl.ds(nodes[step], 1), :] = held[step]
        return carry

    lax.fori_loop(0, layer_rows.shape[0] // LAYER_UNROLL, layer, 0)

    def fold(part, carry):
        for tile in range(own // LANES):
            start = aligned(part * own + tile * LANES)
            block = total[pl.ds(start, LANES), 0:SLOTS].T
            out_ref[part, :, tile * LANES : (tile + 1) * LANES] = (
                block[0:3] + block[3:6] + block[6:9]
            )
        return carry

    lax.fori_loop(0, owners, fold, 0)


def in_smem():
    return pl.BlockSpec(memory_space=pltpu.SMEM)


def in_vmem():
    return pl.BlockSpec(memory_space=pltpu.VMEM)


def in_any():
    return pl.BlockSpec(memory_space=pl.ANY)


def gather_elements(live, layer_ids, corner_ids, disp, shear, lame, scale):
    owners, _, own = disp.shape
    slots = corner_ids.shape[2]
    layers = layer_ids.shape[1]
    return pl.pallas_call(
        gather_kernel,
        out_shape=(
            jax.ShapeDtypeStruct((slots // LANES, SLOTS, LANES), jnp.float32),
            jax.ShapeDtypeStruct((3, layers), jnp.float32),
        ),
        in_specs=[in_smem(), in_smem(), in_any()] + [in_vmem()] * 4,
        out_specs=(in_vmem(), in_vmem()),
        scratch_shapes=[
            pltpu.VMEM((owners * own, LANES), jnp.float32),
            pltpu.VMEM((slots, LANES), jnp.float32),
            pltpu.VMEM((layers, LANES), jnp.float32),
        ]
        + [pltpu.SMEM((slots,), jnp.int32)] * 8
        + [pltpu.SemaphoreType.DMA((8,))],
        compiler_params=pltpu.CompilerParams(vmem_limit_bytes=VMEM_LIMIT),
        cost_estimate=pl.CostEstimate(
            flops=200_000_000, bytes_accessed=180_000_000, transcendentals=0
        ),
        name="corner_gather",
    )(live, layer_ids, corner_ids, disp, shear, lame, scale)


def scatter_forces(live, layer_ids, slot_index, corner_ids, stress, layer_term, replies, owners, own):
    slots = corner_ids.shape[2]
    layers = layer_ids.shape[1]
    return pl.pallas_call(
        scatter_kernel,
        out_shape=jax.ShapeDtypeStruct((owners, 3, own), jnp.float32),
        in_specs=[in_smem(), in_smem(), in_smem(), in_any()] + [in_vmem()] * 3,
        out_specs=in_vmem(),
        scratch_shapes=[
            pltpu.VMEM((owners * own, LANES), jnp.float32),
            pltpu.VMEM((slots, LANES), jnp.float32),
            pltpu.VMEM((layers, LANES), jnp.float32),
            pltpu.VMEM((replies.shape[1], LANES), jnp.float32),
        ]
        + [pltpu.SMEM((slots,), jnp.int32)] * 8
        + [pltpu.SemaphoreType.DMA((8,))],
        compiler_params=pltpu.CompilerParams(vmem_limit_bytes=VMEM_LIMIT),
        cost_estimate=pl.CostEstimate(
            flops=200_000_000, bytes_accessed=250_000_000, transcendentals=0
        ),
        name="force_scatter",
    )(live, layer_ids, slot_index, corner_ids, stress, layer_term, replies)


def stencil_kernel(now, before, factor, x_low, x_high, y_low, y_high, out):
    planes, rows, cols = now.shape[1:]

    def plane(index):
        if index < 0:
            return x_low[0, index + 2]
        if index >= planes:
            return x_high[0, index - planes]
        return now[0, index]

    row = lax.broadcasted_iota(jnp.int32, (rows, cols), 0)
    col = lax.broadcasted_iota(jnp.int32, (rows, cols), 1)
    for index in range(planes):
        here = plane(index)
        low, high = y_low[0, index], y_high[0, index]
        down1 = jnp.where(row == 0, low[1:2], pltpu.roll(here, 1, 0))
        down2 = jnp.where(row == 0, low[0:1], jnp.where(row == 1, low[1:2], pltpu.roll(here, 2, 0)))
        up1 = jnp.where(row == rows - 1, high[0:1], pltpu.roll(here, rows - 1, 0))
        up2 = jnp.where(
            row == rows - 1,
            high[1:2],
            jnp.where(row == rows - 2, high[0:1], pltpu.roll(here, rows - 2, 0)),
        )
        left1 = jnp.where(col == 0, 0.0, pltpu.roll(here, 1, 1))
        left2 = jnp.where(col < 2, 0.0, pltpu.roll(here, 2, 1))
        right1 = jnp.where(col == cols - 1, 0.0, pltpu.roll(here, cols - 1, 1))
        right2 = jnp.where(col >= cols - 2, 0.0, pltpu.roll(here, cols - 2, 1))
        near = (plane(index - 1) + plane(index + 1)) + (down1 + up1) + (left1 + right1)
        far = (plane(index - 2) + plane(index + 2)) + (down2 + up2) + (left2 + right2)
        laplace = (16.0 / 12.0) * near - (1.0 / 12.0) * far - 7.5 * here
        out[0, index] = 2.0 * here - before[0, index] + factor[index] * laplace


def advance(now, before, factor, halos):
    comps, planes, rows, cols = now.shape
    block = pl.BlockSpec((1, planes, rows, cols), lambda c: (c, 0, 0, 0))
    x_side = pl.BlockSpec((1, 2, rows, cols), lambda c: (c, 0, 0, 0))
    y_side = pl.BlockSpec((1, planes, 2, cols), lambda c: (c, 0, 0, 0))
    return pl.pallas_call(
        stencil_kernel,
        grid=(comps,),
        out_shape=jax.ShapeDtypeStruct(now.shape, jnp.float32),
        in_specs=[
            block,
            block,
            pl.BlockSpec((planes, rows, cols), lambda c: (0, 0, 0)),
            x_side,
            x_side,
            y_side,
            y_side,
        ],
        out_specs=block,
        compiler_params=pltpu.CompilerParams(vmem_limit_bytes=VMEM_LIMIT),
        cost_estimate=pl.CostEstimate(
            flops=30_000_000, bytes_accessed=30_000_000, transcendentals=0
        ),
        name="wave_step",
    )(now, before, factor, *halos)


def exchange(field):
    halos = []
    for axis, dim in (("gx", 1), ("gy", 2)):
        count = lax.axis_size(axis)
        forward = [(i, i + 1) for i in range(count - 1)]
        backward = [(target, source) for source, target in forward]
        last = lax.slice_in_dim(field, field.shape[dim] - 2, None, axis=dim)
        first = lax.slice_in_dim(field, 0, 2, axis=dim)
        halos += [lax.ppermute(last, axis, forward), lax.ppermute(first, axis, backward)]
    return halos


def motion_kernel(wanted, field, out):
    lane = lax.broadcasted_iota(jnp.int32, (1, LANES), 1)

    def group(part, carry):
        def step(chunk, held):
            held = list(held)
            for inner in range(8):
                position = chunk * 8 + inner
                cell = wanted[part * LANES + position]
                row = cell >> 7
                shift = (position - cell) & (LANES - 1)
                for comp in range(3):
                    values = field[comp, pl.ds(row, 1), :]
                    held[comp] = jnp.where(
                        lane == position, pltpu.roll(values, shift, 1), held[comp]
                    )
            return tuple(held)

        zero = jnp.zeros((1, LANES), jnp.float32)
        held = lax.fori_loop(0, LANES // 8, step, (zero, zero, zero))
        for comp in range(3):
            out[part, pl.ds(comp, 1), :] = held[comp]
        return carry

    lax.fori_loop(0, out.shape[0], group, 0)


def gather_motion(wanted, field):
    count = wanted.shape[0]
    comps, planes, rows, cols = field.shape
    tiles = field.reshape(comps, planes, rows // 8, 8, cols // LANES, LANES)
    field = jnp.transpose(tiles, (0, 1, 2, 4, 3, 5)).reshape(comps, -1, LANES)
    plane, row, col = wanted // (rows * cols), wanted // cols % rows, wanted % cols
    tile = (plane * (rows // 8) + row // 8) * (cols // LANES) + col // LANES
    wanted = (tile * 8 + row % 8) * LANES + col % LANES
    return pl.pallas_call(
        motion_kernel,
        out_shape=jax.ShapeDtypeStruct((count // LANES, 3, LANES), jnp.float32),
        in_specs=[in_smem(), in_vmem()],
        out_specs=in_vmem(),
        compiler_params=pltpu.CompilerParams(vmem_limit_bytes=VMEM_LIMIT),
        name="motion_gather",
    )(wanted, field)


def on_device(
    grid_now,
    grid_before,
    wave_factor,
    layer_owner,
    layer_cell,
    box_now,
    box_before,
    node_mass,
    corner_nodes,
    live_counts,
    shear_modulus,
    lame_lambda,
    strain_scale,
    layer_nodes,
):
    own_disp = box_now.reshape(3, -1)
    own = own_disp.shape[1]
    all_disp = lax.all_gather(own_disp, "gy", axis=0, tiled=False)
    first_halos = exchange(grid_now)

    owners = layer_owner.reshape(-1)
    cell_index = layer_cell.reshape(-1)
    count_gx = lax.axis_size("gx")
    count_gy = lax.axis_size("gy")
    devices = count_gx * count_gy
    capacity = 2 * owners.shape[0] // devices
    rank_rows = jnp.arange(owners.shape[0])
    earlier = (rank_rows[None, :] < rank_rows[:, None]).astype(jnp.bfloat16)
    matches = owners[:, None] == jnp.arange(devices)[None, :]
    before = jnp.dot(earlier, matches.astype(jnp.bfloat16), preferred_element_type=jnp.float32)
    position = jnp.sum(jnp.where(matches, before, 0.0), axis=1).astype(jnp.int32)
    slot_index = owners * capacity + position
    requests = (
        jnp.zeros((devices * capacity,), jnp.int32)
        .at[slot_index]
        .set(cell_index, unique_indices=True)
    )
    wanted = lax.all_to_all(
        requests.reshape(devices, capacity), ("gx", "gy"), split_axis=0, concat_axis=0, tiled=True
    )

    grid_mid = advance(grid_now, grid_before, wave_factor, first_halos)
    second_halos = exchange(grid_mid)
    stress, layer_term = gather_elements(
        live_counts, layer_nodes, corner_nodes, all_disp, shear_modulus, lame_lambda, strain_scale
    )
    grid_after = advance(grid_mid, grid_now, wave_factor, second_halos)
    moved = gather_motion(wanted.reshape(-1), grid_after)
    moved = jnp.transpose(moved, (1, 0, 2)).reshape(3, devices, capacity)
    returned = lax.all_to_all(moved, ("gx", "gy"), split_axis=1, concat_axis=1, tiled=True)
    node_term = scatter_forces(
        live_counts,
        layer_nodes,
        slot_index.reshape(1, -1),
        corner_nodes,
        stress,
        layer_term,
        returned.reshape(3, devices * capacity),
        count_gy,
        own,
    )
    parts = lax.all_to_all(node_term, "gy", split_axis=0, concat_axis=0, tiled=True)
    summed = jnp.sum(parts, axis=0)
    box_after = 2.0 * own_disp - box_before.reshape(3, -1) + STEP_SQUARE / node_mass * summed
    return (grid_after, box_after.reshape(box_now.shape))


def solution(mesh):
    return jax.shard_map(
        on_device,
        mesh=mesh,
        in_specs=(
            P(None, "gx", "gy", None),
            P(None, "gx", "gy", None),
            P("gx", "gy", None),
            P("gx", "gy", None),
            P("gx", "gy"),
            P(None, "gx", "gy"),
            P(None, "gx", "gy"),
            P("gx", "gy"),
            P(None, "gx", "gy"),
            P("gx", "gy"),
            P("gx", "gy"),
            P("gx", "gy"),
            P("gx", "gy"),
            P("gx", "gy"),
        ),
        out_specs=(P(None, "gx", "gy", None), P(None, "gx", "gy")),
        check_vma=False,
    )
```

time: 1390 us -> 318 us (0.23)
  other arithmetic: 584 us -> 5.98 us
  local copies, waits for them, and re-layouts: 382 us -> 16.3 us
  waiting for transfers between devices: 189 us -> 22.2 us
  Pallas kernels: 0 us -> 160 us
  blocking collectives: 156 us -> 13.8 us
  starting transfers between devices: 55.8 us -> 93.3 us
  between operations: 15.8 us -> 1.57 us
    scatter-add x9 -> x0, other arithmetic: 534 us -> none  [the longest x8 503 us: on_device(): node_term.at[:, corner_ids[corner]]]
    gather x2 -> x0, local copies, waits for them, and re-layouts: 252 us -> none  [the longest x1 227 us: on_device(): jnp.take(all_disp, corner_ids.reshape(-1), axis=1, mode='clip')]
    unnamed x2 -> x0, waiting for transfers between devices: 181 us -> none
    pallas_call x0 -> x5, Pallas kernels: none -> 160 us  [the longest x1 80.2 us: scatter_forces(): pl.pallas_call(scatter_kernel, out_shape=jax.ShapeDtypeStruct((owners, 3,...]
    all_gather x1, blocking collectives: 156 us -> 13.8 us  [on_device(): all_disp = lax.all_gather(own_disp, 'gy', axis=0, tiled=False)]
    add x1 -> x0, local copies, waits for them, and re-layouts: 63.8 us -> none  [advance(): 2.0 * current - previous]
    all_to_all x1 -> x2, starting transfers between devices: 20.4 us -> 62.5 us  [the longest x1 51.1 us: on_device(): lax.all_to_all(node_term, 'gy', split_axis=0, concat_axis=0, tiled=True)]
    add x2 -> x3, other arithmetic: 23.6 us -> 2.06 us  [the longest x1 0.84 us: on_device(): 2.0 * own_disp - box_before.reshape(3, -1)]
  transfers between devices with their start and end apart: 11 -> 11, of which waited for: 3 -> 3; matrix products, arithmetic and copies ran while one was open for 59% -> 5% of each run, Pallas kernels for 0% -> 15%
where the time goes in v1:
time: 318 us; the launch traced here: 314 us
  Pallas kernels  160 us (50%)
  starting transfers between devices  93.3 us (29%)
  waiting for transfers between devices  22.2 us (7%)
  local copies, waits for them, and re-layouts  16.3 us (5%)
  blocking collectives  13.8 us (4%)
  other arithmetic  5.98 us (2%)
    pallas_call x1, Pallas kernels, scatter_forces(): pl.pallas_call(scatter_kernel, out_shape=jax.ShapeDtypeStruct((owners, 3,...  80.2 us
    all_to_all x1, starting transfers between devices, on_device(): lax.all_to_all(node_term, 'gy', split_axis=0, concat_axis=0, tiled=True)  51.1 us
    pallas_call x1, Pallas kernels, gather_elements(): pl.pallas_call(gather_kernel, out_shape=(jax.ShapeDtypeStruct((slots // L...  48.6 us
    all_to_all x1, waiting for transfers between devices, on_device(): lax.all_to_all(node_term, 'gy', split_axis=0, concat_axis=0, tiled=True)  16.9 us
    pallas_call x2, Pallas kernels, advance(): pl.pallas_call(stencil_kernel, grid=(comps,), out_shape=jax.ShapeDtypeStr...  16.5 us
    pallas_call x1, Pallas kernels, gather_motion(): pl.pallas_call(motion_kernel, out_shape=jax.ShapeDtypeStruct((count // LA...  15 us
    all_gather x1, blocking collectives, on_device(): all_disp = lax.all_gather(own_disp, 'gy', axis=0, tiled=False)  13.8 us
    all_to_all x1, starting transfers between devices, on_device(): lax.all_to_all(requests.reshape(devices, capacity), ('gx', 'gy'), split_a...  12.8 us
  transfers between devices with their start and end apart: 11, of which 3 were waited for; matrix products, arithmetic and copies ran while one was open for 5% of the time, Pallas kernels for 15%

profile of v1, /device:TPU:4, one launch (start us, length us, event | category | flops | bytes accessed | tf_op | source)
XLA Modules:
  0.0 314.3 jit_solution(8646376863219443264)
XLA Ops:
  0.6 0.0 copy-start.9
  0.6 0.0 copy-start
  0.7 1.2 fusion.27
  1.9 3.1 collective-permute-start
  5.0 2.7 collective-permute-start.1
  7.7 2.3 fusion.26
  10.0 2.0 collective-permute-start.2
  12.0 1.3 collective-permute-start.3
  13.3 1.1 fusion
  14.4 0.7 compare_select_fusion
  15.1 2.6 scatter_custom_fusion
  17.7 0.7 all_to_all.12
  18.4 12.8 %all-to-all-start = ((s32[128,1,8]{2,1,0:T(1,128)}), s32[128,1,8]{2,1,0:T(1,128)S(1)}, u32[]{:S(2)}, u32[]{:S(2)}) async-start(s32[128,1,8]{2,1,0:T(1,128)} %bitcast.7), calls=%async_computation | async-start | bytes 131072 | tf_op jit(solution)/shard_map/all_to_all | solution.py:421
  31.2 0.0 copy-done
  31.2 13.8 %all-gather = f32[24,1,8960]{2,1,0:T(1,128)S(1)} all-gather(f32[3,1,8960]{2,1,0:T(1,128)S(1)} %copy-done), channel_id=2, replica_groups=mesh['gx'=16,'gy'=8] {'gy'}, dimensions={0}, use_global_device_ids=true | all-gather | bytes 967680 | tf_op jit(solution)/shard_map/all_gather | solution.py:401
  45.0 0.0 copy-done.9
  45.0 0.6 bitcast_add_fusion.1.slot_ref
  46.3 2.1 reduce.1
  48.4 1.4 reshape.133.disp_ref
  49.8 0.0 all-to-all-done
  49.8 0.5 broadcast.95
  50.3 0.8 reduce.6
  51.1 0.1 reshape.120
  51.2 0.0 collective-permute-done.2.y_low
  51.2 0.0 collective-permute-done.3.y_high
  51.2 0.0 collective-permute-done.x_low
  51.2 0.0 copy-start.1
  51.2 0.0 collective-permute-done.1.x_high
  51.3 0.7 copy-done.1
  52.0 0.8 copy-done.2
  52.7 8.2 %wave_step.2.now = f32[3,16,32,512]{3,2,1,0:T(8,128)} custom-call(f32[3,16,32,512]{3,2,1,0:T(8,128)} %before.3, f32[3,16,32,512]{3,2,1,0:T(8,128)} %before.2, f32[16,32,512]{2,1,0:T(8,128)} %factor.3, f32[3,2,32,512]{3,2,1,0:T(8,128)} %copy-done.1, f32[3,2,32,512]{3,2,1,0:T(8,128)} %copy-done.2, f32[3,16,2,512]{3,2,1,0:T(2,128)} %collective-permute-done.2.y_low, ...), custom_call_target="tpu_custom_call" | custom-call | flops 30000000 | bytes 30000000 | tf_op jit(solution)/shard_map/wave_step/pallas_call | solution.py:304
  61.0 1.2 fusion.25
  62.2 3.1 collective-permute-start.4
  65.3 2.7 collective-permute-start.5
  68.0 1.6 fusion.24
  69.6 1.7 collective-permute-start.6
  71.3 1.3 collective-permute-start.7
  72.6 0.6 fusion.10.wanted
  73.2 0.0 collective-permute-done.6.y_low
  73.2 2.6 collective-permute-done.7.y_high
  75.8 0.0 collective-permute-done.4.x_low
  75.8 2.6 collective-permute-done.5.x_high
  78.5 0.0 copy-done.5
  78.5 0.0 copy-done.6
  78.5 0.0 copy-done.3
  78.5 0.8 copy-done.4
  79.2 8.2 %wave_step.3 = f32[3,16,32,512]{3,2,1,0:T(8,128)} custom-call(f32[3,16,32,512]{3,2,1,0:T(8,128)} %wave_step.2.now, f32[3,16,32,512]{3,2,1,0:T(8,128)} %before.3, f32[16,32,512]{2,1,0:T(8,128)} %factor.3, f32[3,2,32,512]{3,2,1,0:T(8,128)} %copy-done.3, f32[3,2,32,512]{3,2,1,0:T(8,128)} %copy-done.4, f32[3,16,2,512]{3,2,1,0:T(2,128)} %copy-done.5, ...), custom_call_target="tpu_custom_call" | custom-call | flops 30000000 | bytes 30000000 | tf_op jit(solution)/shard_map/wave_step/pallas_call | solution.py:304
  87.5 15.0 %motion_gather.1 = f32[8,3,128]{2,1,0:T(4,128)} custom-call(s32[1024]{0:T(1024)} %fusion.10.wanted, f32[3,2048,128]{2,1,0:T(8,128)} %bitcast.18), custom_call_target="tpu_custom_call" | custom-call | tf_op jit(solution)/shard_map/motion_gather/pallas_call | solution.py:373
  102.5 0.7 copy.18
  103.2 0.1 reshape.123
  103.3 0.8 copy.19
  104.2 11.4 %all-to-all-start.1 = ((f32[3,128,8]{2,0,1:T(4,128)}), f32[3,128,8]{2,0,1:T(4,128)S(1)}, u32[]{:S(2)}, u32[]{:S(2)}) async-start(f32[3,128,8]{2,0,1:T(4,128)} %copy.19), calls=%async_computation.1 | async-start | bytes 524288 | tf_op jit(solution)/shard_map/all_to_all | solution.py:433
  115.5 0.0 copy-start.8
  115.5 48.6 %corner_gather.1 = (f32[64,16,128]{2,1,0:T(8,128)}, f32[3,512]{1,0:T(4,128)}) custom-call(s32[1,1]{1,0:T(1,128)S(6)} %copy.22.live_ref, s32[1,512]{1,0:T(1,128)} %layer_ref.3, s32[8,1,8192]{2,1,0:T(1,128)} %corner_hbm.3, f32[8,3,8960]{2,1,0:T(4,128)} %reshape.133.disp_ref, f32[1,8192]{1,0:T(1,128)} %shear_ref.1, f32[1,8192]{1,0:T(1,128)} %lame_ref.1, ...), custom_call_target="tpu_custom_call" | custom-call | flops 200000000 | bytes 180000000 | tf_op jit(solution)/shard_map/corner_gather/pallas_call | solution.py:219
  164.1 0.0 copy-start.7
  164.1 0.0 all-to-all-done.1
  164.2 0.7 reshape.124.reply_ref
  164.9 80.2 %force_scatter.1 = f32[8,3,8960]{2,1,0:T(4,128)} custom-call(s32[1,1]{1,0:T(1,128)S(6)} %copy.22.live_ref, s32[1,512]{1,0:T(1,128)} %layer_ref.3, s32[1,512]{1,0:T(1,128)} %bitcast_add_fusion.1.slot_ref, s32[8,1,8192]{2,1,0:T(1,128)} %corner_hbm.3, f32[64,16,128]{2,1,0:T(8,128)} %get-tuple-element.4.stress_ref, f32[3,512]{1,0:T(4,128)} %get-tuple-element.5.layer_in, ...), custom_call_target="tpu_custom_call" | custom-call | flops 200000000 | bytes 250000000 | tf_op jit(solution)/shard_map/force_scatter/pallas_call | solution.py:245
  245.1 51.1 %all-to-all-start.2 = ((f32[8,3,8960]{2,1,0:T(4,128)}), f32[8,3,8960]{2,1,0:T(4,128)S(1)}, u32[]{:S(2)}, u32[]{:S(2)}) async-start(f32[8,3,8960]{2,1,0:T(4,128)} %force_scatter.1), calls=%async_computation.2 | async-start | bytes 2293760 | tf_op jit(solution)/shard_map/all_to_all | solution.py:445
  296.2 0.1 divide_reduce_fusion
  296.3 16.9 %all-to-all-done.2 = f32[8,3,8960]{2,1,0:T(4,128)S(1)} async-done(((f32[8,3,8960]{2,1,0:T(4,128)}), f32[8,3,8960]{2,1,0:T(4,128)S(1)}, u32[]{:S(2)}, u32[]{:S(2)}) %all-to-all-start.2) | async-done | bytes 860192 | tf_op jit(solution)/shard_map/all_to_all | solution.py:445
  313.2 0.2 reduce_sum.21
  313.5 0.0 copy-done.7
  313.5 0.8 multiply_add_fusion
  (8 shorter events, 0.0 us)
Async XLA Ops:
  0.6 44.4 %copy-start.9 = (s32[1,512,1]{1,2,0:T(1,128)S(1)}, s32[1,512,1]{1,2,0:T(1,128)}, u32[]{:S(2)}) copy-start(s32[1,512,1]{1,2,0:T(1,128)} %param.17) | copy-start | bytes 6148
  0.6 30.6 %copy-start = (f32[3,1,8960]{2,1,0:T(1,128)S(1)}, f32[3,1,8960]{2,1,0:T(1,128)}, u32[]{:S(2)}) copy-start(f32[3,1,8960]{2,1,0:T(1,128)} %param.19) | copy-start | bytes 322564
  1.9 49.3 %collective-permute-start = (f32[3,2,32,512]{3,2,1,0:T(8,128)S(1)}, f32[3,2,32,512]{3,2,1,0:T(8,128)S(1)}, u32[]{:S(2)}, u32[]{:S(2)}) collective-permute-start(f32[3,2,32,512]{3,2,1,0:T(8,128)S(1)} %get-tuple-element.13), channel_id=1, source_target_pairs={{0,8},{8,16},{16,24},{24,32},{32,40},{40,48},{48,56},{56,64},{64,7... | collective-permute-start | bytes 1179656 | tf_op jit(solution)/shard_map/ppermute | solution.py:334
  5.0 46.2 %collective-permute-start.1 = (f32[3,2,32,512]{3,2,1,0:T(8,128)S(1)}, f32[3,2,32,512]{3,2,1,0:T(8,128)S(1)}, u32[]{:S(2)}, u32[]{:S(2)}) collective-permute-start(f32[3,2,32,512]{3,2,1,0:T(8,128)S(1)} %get-tuple-element.12), channel_id=1, source_target_pairs={{8,0},{16,8},{24,16},{32,24},{40,32},{48,40},{56,48},{64,56},{72,6... | collective-permute-start | bytes 1179656 | tf_op jit(solution)/shard_map/ppermute | solution.py:334
  10.0 41.2 %collective-permute-start.2 = (f32[3,16,2,512]{3,2,1,0:T(2,128)}, f32[3,16,2,512]{3,2,1,0:T(2,128)}, u32[]{:S(2)}, u32[]{:S(2)}) collective-permute-start(f32[3,16,2,512]{3,2,1,0:T(2,128)} %get-tuple-element.11), channel_id=1, source_target_pairs={{0,1},{1,2},{2,3},{3,4},{4,5},{5,6},{6,7},{8,9},{9,10},{10,11},{11... | collective-permute-start | bytes 589832 | tf_op jit(solution)/shard_map/ppermute | solution.py:334
  12.0 39.2 %collective-permute-start.3 = (f32[3,16,2,512]{3,2,1,0:T(2,128)}, f32[3,16,2,512]{3,2,1,0:T(2,128)}, u32[]{:S(2)}, u32[]{:S(2)}) collective-permute-start(f32[3,16,2,512]{3,2,1,0:T(2,128)} %get-tuple-element.10), channel_id=1, source_target_pairs={{1,0},{2,1},{3,2},{4,3},{5,4},{6,5},{7,6},{9,8},{10,9},{11,10},{12... | collective-permute-start | bytes 589832 | tf_op jit(solution)/shard_map/ppermute | solution.py:334
  18.4 31.4 %all-to-all-start = ((s32[128,1,8]{2,1,0:T(1,128)}), s32[128,1,8]{2,1,0:T(1,128)S(1)}, u32[]{:S(2)}, u32[]{:S(2)}) async-start(s32[128,1,8]{2,1,0:T(1,128)} %bitcast.7), calls=%async_computation | async-start | bytes 131072 | tf_op jit(solution)/shard_map/all_to_all | solution.py:421
  51.2 0.7 copy-start.1
  52.0 0.8 copy-start.2
  62.2 13.7 %collective-permute-start.4 = (f32[3,2,32,512]{3,2,1,0:T(8,128)S(1)}, f32[3,2,32,512]{3,2,1,0:T(8,128)S(1)}, u32[]{:S(2)}, u32[]{:S(2)}) collective-permute-start(f32[3,2,32,512]{3,2,1,0:T(8,128)S(1)} %get-tuple-element.9), channel_id=1, source_target_pairs={{0,8},{8,16},{16,24},{24,32},{32,40},{40,48},{48,56},{56,64},{64,7... | collective-permute-start | bytes 1179656 | tf_op jit(solution)/shard_map/ppermute | solution.py:334
  65.3 13.2 %collective-permute-start.5 = (f32[3,2,32,512]{3,2,1,0:T(8,128)S(1)}, f32[3,2,32,512]{3,2,1,0:T(8,128)S(1)}, u32[]{:S(2)}, u32[]{:S(2)}) collective-permute-start(f32[3,2,32,512]{3,2,1,0:T(8,128)S(1)} %get-tuple-element.8), channel_id=1, source_target_pairs={{8,0},{16,8},{24,16},{32,24},{40,32},{48,40},{56,48},{64,56},{72,6... | collective-permute-start | bytes 1179656 | tf_op jit(solution)/shard_map/ppermute | solution.py:334
  69.6 3.6 %collective-permute-start.6 = (f32[3,16,2,512]{3,2,1,0:T(2,128)S(1)}, f32[3,16,2,512]{3,2,1,0:T(2,128)S(1)}, u32[]{:S(2)}, u32[]{:S(2)}) collective-permute-start(f32[3,16,2,512]{3,2,1,0:T(2,128)S(1)} %get-tuple-element.7), channel_id=1, source_target_pairs={{0,1},{1,2},{2,3},{3,4},{4,5},{5,6},{6,7},{8,9},{9,10},{10,11},{11... | collective-permute-start | bytes 589832 | tf_op jit(solution)/shard_map/ppermute | solution.py:334
  71.3 4.5 %collective-permute-start.7 = (f32[3,16,2,512]{3,2,1,0:T(2,128)S(1)}, f32[3,16,2,512]{3,2,1,0:T(2,128)S(1)}, u32[]{:S(2)}, u32[]{:S(2)}) collective-permute-start(f32[3,16,2,512]{3,2,1,0:T(2,128)S(1)} %get-tuple-element.6), channel_id=1, source_target_pairs={{1,0},{2,1},{3,2},{4,3},{5,4},{6,5},{7,6},{9,8},{10,9},{11,10},{12... | collective-permute-start | bytes 589832 | tf_op jit(solution)/shard_map/ppermute | solution.py:334
  73.2 5.3 %copy-start.5 = (f32[3,16,2,512]{3,2,1,0:T(2,128)}, f32[3,16,2,512]{3,2,1,0:T(2,128)S(1)}, u32[]{:S(2)}) copy-start(f32[3,16,2,512]{3,2,1,0:T(2,128)S(1)} %collective-permute-done.6.y_low) | copy-start | bytes 589828
  75.8 2.6 copy-start.6
  75.8 2.6 copy-start.3
  78.5 0.8 copy-start.4
  104.2 60.0 %all-to-all-start.1 = ((f32[3,128,8]{2,0,1:T(4,128)}), f32[3,128,8]{2,0,1:T(4,128)S(1)}, u32[]{:S(2)}, u32[]{:S(2)}) async-start(f32[3,128,8]{2,0,1:T(4,128)} %copy.19), calls=%async_computation.1 | async-start | bytes 524288 | tf_op jit(solution)/shard_map/all_to_all | solution.py:433
  115.5 180.7 %copy-start.8 = (f32[1,8960]{1,0:T(1,128)S(1)}, f32[1,8960]{1,0:T(1,128)}, u32[]{:S(2)}) copy-start(f32[1,8960]{1,0:T(1,128)} %param.21) | copy-start | bytes 107524
  164.1 149.3 %copy-start.7 = (f32[3,1,8960]{2,1,0:T(1,128)S(1)}, f32[3,1,8960]{2,1,0:T(1,128)}, u32[]{:S(2)}) copy-start(f32[3,1,8960]{2,1,0:T(1,128)} %param.20) | copy-start | bytes 322564
  245.1 68.2 %all-to-all-start.2 = ((f32[8,3,8960]{2,1,0:T(4,128)}), f32[8,3,8960]{2,1,0:T(4,128)S(1)}, u32[]{:S(2)}, u32[]{:S(2)}) async-start(f32[8,3,8960]{2,1,0:T(4,128)} %force_scatter.1), calls=%async_computation.2 | async-start | bytes 2293760 | tf_op jit(solution)/shard_map/all_to_all | solution.py:445

commit v2 on v0

v2 whole, which is shorter than its diff:
```python
import jax
import jax.numpy as jnp
from jax import lax
from jax.experimental import pallas as pl
from jax.experimental.pallas import tpu as pltpu
from jax.sharding import PartitionSpec as P

PENALTY = 2.0
STEP_SQUARE = 0.25
NEAR = 16.0 / 12.0
FAR = -1.0 / 12.0
LANES = 128
SLOTS = 16
ID_ROWS = 72
PLANE = 128
VMEM_LIMIT = 58 * 2**20
GATHER_UNROLL = 16
SCATTER_UNROLL = 2
LAYER_UNROLL = 16
MESH = pl.DeviceIdType.MESH


def aligned(start, unit=LANES):
    return pl.multiple_of(start, unit)


def wave_plane(comp, index, now, before, factor, out, out_shift):
    start = aligned((index + 2) * PLANE)

    def block(offset, group, tile):
        return now[comp, pl.ds(start + offset * PLANE + (group * 4 + tile) * 8, 8), :]

    sub = lax.broadcasted_iota(jnp.int32, (8, LANES), 0)
    lane = lax.broadcasted_iota(jnp.int32, (8, LANES), 1)
    zero = jnp.zeros((8, LANES), jnp.float32)
    here = [[block(0, group, tile) for tile in range(4)] for group in range(4)]

    def neighbours(values, axis, count, position):
        sums = []
        for distance in (1, 2):
            ahead = [pltpu.roll(value, distance, axis) for value in values]
            behind = [pltpu.roll(value, count - distance, axis) for value in values]
            rows = []
            for spot in range(4):
                low = ahead[spot - 1] if spot > 0 else zero
                high = behind[spot + 1] if spot < 3 else zero
                rows.append(
                    jnp.where(position < distance, low, ahead[spot])
                    + jnp.where(position >= count - distance, high, behind[spot])
                )
            sums.append(rows)
        return sums

    along_y = [neighbours([here[g][t] for g in range(4)], 0, 8, sub) for t in range(4)]
    along_z = [neighbours(here[g], 1, LANES, lane) for g in range(4)]
    for group in range(4):
        for tile in range(4):
            row = (group * 4 + tile) * 8
            near = block(-1, group, tile) + block(1, group, tile)
            far = block(-2, group, tile) + block(2, group, tile)
            near = near + (along_y[tile][0][group] + along_z[group][0][tile])
            far = far + (along_y[tile][1][group] + along_z[group][1][tile])
            centre = here[group][tile]
            laplace = NEAR * near + FAR * far - 7.5 * centre
            place = pl.ds(aligned(index * PLANE) + row, 8)
            result = 2.0 * centre - before[comp, pl.ds(aligned(before_start(before, index)) + row, 8), :]
            out[comp, pl.ds(aligned((index + out_shift) * PLANE) + row, 8), :] = (
                result + factor[place, :] * laplace
            )


def before_start(before, index):
    shift = 2 if before.shape[1] == 20 * PLANE else 0
    return (index + shift) * PLANE


def y_edges(comp, index, source, low_out, high_out):
    start = aligned((index + 2) * PLANE)
    for tile in range(4):
        first = source[comp, pl.ds(start + tile * 8, 8), :]
        last = source[comp, pl.ds(start + 96 + tile * 8, 8), :]
        low_out[comp, index, 2 * tile : 2 * tile + 2, :] = first[0:2]
        high_out[comp, index, 2 * tile : 2 * tile + 2, :] = last[6:8]


def y_corrections(comp, index, low, high, low_weight, high_weight, factor, out, out_shift):
    sub = lax.broadcasted_iota(jnp.int32, (8, LANES), 0)
    start = aligned((index + out_shift) * PLANE)
    here = aligned(index * PLANE)
    lows = low[comp, index] * low_weight
    highs = high[comp, index] * high_weight
    for tile in range(4):
        far_row, near_row = lows[2 * tile : 2 * tile + 1], lows[2 * tile + 1 : 2 * tile + 2]
        term = jnp.where(
            sub == 0, NEAR * near_row + FAR * far_row, jnp.where(sub == 1, FAR * near_row, 0.0)
        )
        place = pl.ds(start + tile * 8, 8)
        out[comp, place, :] = out[comp, place, :] + factor[pl.ds(here + tile * 8, 8), :] * term
        near_row, far_row = highs[2 * tile : 2 * tile + 1], highs[2 * tile + 1 : 2 * tile + 2]
        term = jnp.where(
            sub == 7, NEAR * near_row + FAR * far_row, jnp.where(sub == 6, FAR * near_row, 0.0)
        )
        place = pl.ds(start + 96 + tile * 8, 8)
        out[comp, place, :] = out[comp, place, :] + factor[pl.ds(here + 96 + tile * 8, 8), :] * term


def grid_kernel(
    now_hbm, before_hbm, factor_hbm, request, disp_hbm, ids_hbm, params_hbm,
    after_hbm, disp_all, ids_all, params_all, reply_out,
    now, mid, after, before, factor, y_sent, y_got, asked_x, asked_t, asked_y, rows_vmem,
    rows_smem, found, found_x, found_t, send_sems, recv_sems, local_sems,
):
    gx, gy = lax.axis_index("gx"), lax.axis_index("gy")
    count_x, count_y = lax.axis_size("gx"), lax.axis_size("gy")
    planes = factor.shape[0] // PLANE
    edge = 2 * PLANE
    inside = pl.ds(edge, planes * PLANE)

    loads = [
        pltpu.make_async_copy(now_hbm, now.at[:, inside, :], local_sems.at[0]),
        pltpu.make_async_copy(before_hbm, before, local_sems.at[1]),
        pltpu.make_async_copy(factor_hbm, factor, local_sems.at[2]),
    ]
    for load in loads:
        load.start()

    barrier = pltpu.get_barrier_semaphore()
    for step in range(1, count_x):
        peer = lax.rem(gx + step, count_x)
        pl.semaphore_signal(barrier, inc=1, device_id=(peer, gy), device_id_type=MESH)
    for step in range(1, count_y):
        peer = lax.rem(gy + step, count_y)
        pl.semaphore_signal(barrier, inc=1, device_id=(gx, peer), device_id_type=MESH)
    pl.semaphore_wait(barrier, count_x + count_y - 2)

    used = [0]

    def send(source, target, device):
        slot = used[0]
        used[0] += 1
        copy = pltpu.make_async_remote_copy(
            src_ref=source,
            dst_ref=target,
            send_sem=send_sems.at[slot],
            recv_sem=recv_sems.at[slot],
            device_id=device,
            device_id_type=MESH,
        )
        copy.start()
        return copy

    right, left = lax.rem(gx + 1, count_x), lax.rem(gx + count_x - 1, count_x)
    upper, lower = lax.rem(gy + 1, count_y), lax.rem(gy + count_y - 1, count_y)
    top = (planes - 2) * PLANE

    def x_halo(source, shift, target):
        return [
            send(
                source.at[:, pl.ds(top + shift, edge), :],
                target.at[:, pl.ds(0, edge), :],
                (right, gy),
            ),
            send(
                source.at[:, pl.ds(shift, edge), :],
                target.at[:, pl.ds(edge + planes * PLANE, edge), :],
                (left, gy),
            ),
        ]

    def y_halo(step):
        return [
            send(y_sent.at[step, 1], y_got.at[step, 0], (gx, upper)),
            send(y_sent.at[step, 0], y_got.at[step, 1], (gx, lower)),
        ]

    def each_plane(indices, body):
        def run(comp, carry):
            for low, high in indices:
                lax.fori_loop(low, high, lambda index, c: (body(comp, index), c)[1], 0)
            return carry

        lax.fori_loop(0, 3, run, 0)

    def edges(step, source):
        each_plane(
            [(0, planes)],
            lambda comp, index: y_edges(comp, index, source, y_sent.at[step, 0], y_sent.at[step, 1]),
        )

    def clear_outside(target):
        @pl.when(gx == 0)
        def _():
            target[:, 0:edge, :] = jnp.zeros((3, edge, LANES), jnp.float32)

        @pl.when(gx == count_x - 1)
        def _():
            target[:, edge + planes * PLANE :, :] = jnp.zeros((3, edge, LANES), jnp.float32)

    low_weight = jnp.where(gy == 0, 0.0, 1.0).astype(jnp.float32)
    high_weight = jnp.where(gy == count_y - 1, 0.0, 1.0).astype(jnp.float32)

    first_x = x_halo(now_hbm, 0, now)
    asks = []
    for step in range(1, count_x):
        peer = lax.rem(gx + step, count_x)
        asks.append(send(request.at[peer], asked_x.at[gx], (peer, gy)))
    asked_x[gx] = request[gx]
    loads[0].wait()
    edges(0, now)
    first_y = y_halo(0)
    bulk = []
    for step in range(1, count_y):
        peer = lax.rem(gy + step, count_y)
        bulk.append(send(disp_hbm, disp_all.at[gy], (gx, peer)))
        bulk.append(send(ids_hbm.at[peer], ids_all.at[gy], (gx, peer)))
        bulk.append(send(params_hbm.at[peer], params_all.at[gy], (gx, peer)))
    own = [
        pltpu.make_async_copy(disp_hbm, disp_all.at[gy], local_sems.at[3]),
        pltpu.make_async_copy(ids_hbm.at[gy], ids_all.at[gy], local_sems.at[4]),
        pltpu.make_async_copy(params_hbm.at[gy], params_all.at[gy], local_sems.at[5]),
    ]
    for copy in own:
        copy.start()
    loads[1].wait()
    loads[2].wait()

    def step_of(source, previous, target, shift):
        return lambda comp, index: wave_plane(comp, index, source, previous, factor, target, shift)

    def fix(step, target, shift):
        each_plane(
            [(0, planes)],
            lambda comp, index: y_corrections(
                comp, index, y_got.at[step, 0], y_got.at[step, 1], low_weight, high_weight,
                factor, target, shift,
            ),
        )

    inner, outer = [(2, planes - 2)], [(0, 2), (planes - 2, planes)]
    first = step_of(now, before, mid, 2)
    each_plane(inner, first)
    for copy in asks:
        copy.wait()
    for peer in range(count_y):
        asked_t[peer] = asked_x[:, peer, :]
    passes = []
    for step in range(1, count_y):
        peer = lax.rem(gy + step, count_y)
        passes.append(send(asked_t.at[peer], asked_y.at[gy], (gx, peer)))
    asked_y[gy] = asked_t[gy]
    for copy in first_x:
        copy.wait()
    clear_outside(now)
    each_plane(outer, first)
    for copy in first_y:
        copy.wait()
    fix(0, mid, 2)

    second_x = x_halo(mid, edge, mid)
    edges(1, mid)
    second_y = y_halo(1)
    second = step_of(mid, now, after, 0)
    each_plane(inner, second)
    for copy in passes:
        copy.wait()
    cell = asked_y[...]
    plane, row, col = cell >> 14, (cell >> 9) & 31, cell & 511
    rows_vmem[...] = (((plane * 4 + (row >> 3)) * 4 + (col >> 7)) * 8 + (row & 7)) * LANES + (
        col & (LANES - 1)
    )
    to_smem = pltpu.make_async_copy(rows_vmem, rows_smem, local_sems.at[6])
    to_smem.start()
    for copy in second_x:
        copy.wait()
    clear_outside(mid)
    each_plane(outer, second)
    for copy in second_y:
        copy.wait()
    fix(1, after, 0)
    store = pltpu.make_async_copy(after, after_hbm, local_sems.at[7])
    store.start()
    to_smem.wait()

    lane = lax.broadcasted_iota(jnp.int32, (1, LANES), 1)
    capacity = LANES // SLOTS

    def find(source, carry):
        for part in range(count_y):
            held = jnp.zeros((1, LANES), jnp.float32)
            for position in range(capacity):
                place = rows_smem[part, source, position]
                line = place >> 7
                for comp in range(3):
                    spot = position * SLOTS + comp
                    values = after[comp, pl.ds(line, 1), :]
                    shift = (spot - place) & (LANES - 1)
                    held = jnp.where(lane == spot, pltpu.roll(values, shift, 1), held)
            found[part, pl.ds(source, 1), :] = held
        return carry

    lax.fori_loop(0, count_x, find, 0)
    answers = []
    for step in range(1, count_y):
        peer = lax.rem(gy + step, count_y)
        answers.append(send(found.at[peer], found_x.at[gy], (gx, peer)))
    found_x[gy] = found[gy]
    for copy in answers:
        copy.wait()
    for peer in range(count_x):
        found_t[peer] = found_x[:, peer, :]
    finals = []
    for step in range(1, count_x):
        peer = lax.rem(gx + step, count_x)
        finals.append(send(found_t.at[peer], reply_out.at[gx], (peer, gy)))
    reply_out[gx] = found_t[gx]
    for copy in finals + bulk + own:
        copy.wait()
    store.wait()


def grid_steps(now, before, factor, request, disp, ids, params, count_x, count_y):
    rows = factor.shape[0]
    f32, i32 = jnp.float32, jnp.int32
    hbm = pl.BlockSpec(memory_space=pl.ANY)
    vmem = pl.BlockSpec(memory_space=pltpu.VMEM)
    halo_rows = rows + 4 * PLANE
    copies = 8 + 3 * (count_y - 1) + 2 * (count_x - 1) + 2 * (count_y - 1)
    planes = rows // PLANE
    return pl.pallas_call(
        grid_kernel,
        out_shape=(
            jax.ShapeDtypeStruct(now.shape, f32),
            jax.ShapeDtypeStruct((count_y,) + disp.shape, f32),
            jax.ShapeDtypeStruct(ids.shape, i32),
            jax.ShapeDtypeStruct(params.shape, f32),
            jax.ShapeDtypeStruct(request.shape, f32),
        ),
        in_specs=[hbm, hbm, hbm, vmem, hbm, hbm, hbm],
        out_specs=(hbm, hbm, hbm, hbm, vmem),
        scratch_shapes=[
            pltpu.VMEM((3, halo_rows, LANES), f32),
            pltpu.VMEM((3, halo_rows, LANES), f32),
            pltpu.VMEM((3, rows, LANES), f32),
            pltpu.VMEM((3, rows, LANES), f32),
            pltpu.VMEM((rows, LANES), f32),
            pltpu.VMEM((2, 2, 3, planes, 8, LANES), f32),
            pltpu.VMEM((2, 2, 3, planes, 8, LANES), f32),
            pltpu.VMEM((count_x, count_y, LANES), i32),
            pltpu.VMEM((count_y, count_x, LANES), i32),
            pltpu.VMEM((count_y, count_x, LANES), i32),
            pltpu.VMEM((count_y, count_x, LANES), i32),
            pltpu.SMEM((count_y, count_x, LANES), i32),
            pltpu.VMEM((count_y, count_x, LANES), f32),
            pltpu.VMEM((count_y, count_x, LANES), f32),
            pltpu.VMEM((count_x, count_y, LANES), f32),
            pltpu.SemaphoreType.DMA((copies,)),
            pltpu.SemaphoreType.DMA((copies,)),
            pltpu.SemaphoreType.DMA((8,)),
        ],
        compiler_params=pltpu.CompilerParams(
            vmem_limit_bytes=VMEM_LIMIT, collective_id=1, has_side_effects=True
        ),
        name="grid_steps",
    )(now, before, factor, request, disp, ids, params)


def gradient_signs(corner):
    lane = lax.broadcasted_iota(jnp.int32, (1, LANES), 1)
    signs = jnp.zeros((1, LANES), jnp.float32)
    for direction in range(3):
        value = 0.25 if (corner >> direction) & 1 else -0.25
        inside = (lane >= 3 * direction) & (lane < 3 * direction + 3)
        signs = jnp.where(inside, value, signs)
    return signs


def rows_of(values):
    count = values.shape[0]
    padded = jnp.concatenate(
        [values, jnp.zeros((SLOTS - count, LANES), jnp.float32)], axis=0
    )
    return padded.T


def box_kernel(
    layer_ref, slot_ref, ids_hbm, disp_ref, params_ref, reply_ref,
    out_ref, table, rows, layer_rows, reply_rows, counts, *rest,
):
    ids, sems, count_sem = rest[:8], rest[8], rest[9]
    owners, _, own = disp_ref.shape
    stripe = ids[0].shape[0] // owners
    span = ID_ROWS * LANES
    copies = []
    for part in range(owners):
        copies.append(
            pltpu.make_async_copy(
                ids_hbm.at[pl.ds(part * span + 8 * stripe, 1024)],
                counts.at[pl.ds(part * 1024, 1024)],
                count_sem.at[part],
            )
        )
        for corner in range(8):
            copies.append(
                pltpu.make_async_copy(
                    ids_hbm.at[pl.ds(part * span + corner * stripe, stripe)],
                    ids[corner].at[pl.ds(part * stripe, stripe)],
                    sems.at[part, corner],
                )
            )
    for copy in copies:
        copy.start()

    def build(part, carry):
        for tile in range(own // LANES):
            block = disp_ref[part, :, tile * LANES : (tile + 1) * LANES]
            lines = rows_of(jnp.concatenate([block, block, block], axis=0))
            table[pl.ds(aligned(part * own + tile * LANES), LANES), 0:SLOTS] = lines
        return carry

    lax.fori_loop(0, owners, build, 0)
    signs = [gradient_signs(corner) for corner in range(8)]
    mine = lax.axis_index("gy")

    def live_of(part):
        count = counts[part * 1024]
        whole = count // LANES
        tiles = (whole + owners - 1 - mine) // owners
        partial = jnp.where(whole % owners == mine, count % LANES, 0)
        return tiles * LANES + partial

    for copy in copies:
        copy.wait()

    for part in range(owners):

        def gather(chunk, carry, part=part):
            base = part * stripe + chunk * GATHER_UNROLL
            for step in range(GATHER_UNROLL):
                slot = base + step
                ends = [table[pl.ds(ids[corner][slot], 1), :] for corner in range(8)]
                spans = [ends[corner] - ends[7 - corner] for corner in range(4)]
                rows[pl.ds(slot, 1), :] = (spans[0] * signs[0] + spans[1] * signs[1]) + (
                    spans[2] * signs[2] + spans[3] * signs[3]
                )
            return carry

        lax.fori_loop(0, (live_of(part) + GATHER_UNROLL - 1) // GATHER_UNROLL, gather, 0)

    def layer_ends(chunk, carry):
        base = chunk * LAYER_UNROLL
        for step in range(LAYER_UNROLL):
            node = layer_ref[0, base + step]
            layer_rows[pl.ds(base + step, 1), :] = table[pl.ds(node, 1), :]
        return carry

    layers = layer_rows.shape[0]
    lax.fori_loop(0, layers // LAYER_UNROLL, layer_ends, 0)

    def clear(chunk, carry):
        zero = jnp.zeros((LANES, LANES), jnp.float32)
        table[pl.ds(aligned(chunk * LANES), LANES), :] = zero
        return carry

    lax.fori_loop(0, table.shape[0] // LANES, clear, 0)
    lane = lax.broadcasted_iota(jnp.int32, (1, LANES), 1)
    total = table
    tiles = stripe // LANES

    for part in range(owners):
        live = live_of(part)

        def element(tile, carry, part=part, live=live):
            start = aligned(part * stripe + tile * LANES)
            grads = rows[pl.ds(start, LANES), 0:SLOTS].T
            slope = [[grads[3 * j + i : 3 * j + i + 1] for j in range(3)] for i in range(3)]
            s00, s11, s22 = slope[0][0], slope[1][1], slope[2][2]
            s01 = 0.5 * (slope[0][1] + slope[1][0])
            s02 = 0.5 * (slope[0][2] + slope[2][0])
            s12 = 0.5 * (slope[1][2] + slope[2][1])
            trace = s00 + s11 + s22
            mean = trace / 3.0
            d00, d11, d22 = s00 - mean, s11 - mean, s22 - mean
            invariant = d00 * d00 + d11 * d11 + d22 * d22
            invariant = invariant + 2.0 * (s01 * s01 + s02 * s02 + s12 * s12)
            shear = params_ref[part, pl.ds(tile, 1), :]
            lame = params_ref[part, pl.ds(tiles + tile, 1), :]
            scale = params_ref[part, pl.ds(2 * tiles + tile, 1), :]
            softened = 2.0 * shear / (1.0 + invariant / scale)
            volume = lame * trace
            index = tile * LANES + lane

            def signed(value):
                return jnp.where(index < live, -value, 0.0)

            p00 = signed(volume + softened * s00)
            p11 = signed(volume + softened * s11)
            p22 = signed(volume + softened * s22)
            p01, p02, p12 = signed(softened * s01), signed(softened * s02), signed(softened * s12)
            rows[pl.ds(start, LANES), 0:SLOTS] = rows_of(
                jnp.concatenate([p00, p01, p02, p01, p11, p12, p02, p12, p22], axis=0)
            )
            return carry

        lax.fori_loop(0, (live + LANES - 1) // LANES, element, 0)

        def scatter(chunk, carry, part=part):
            base = part * stripe + chunk * SCATTER_UNROLL
            for step in range(SCATTER_UNROLL):
                line = rows[pl.ds(base + step, 1), :]
                nodes = [ids[corner][base + step] for corner in range(8)]
                terms = [line * signs[corner] for corner in range(4)]
                held = [total[pl.ds(node, 1), :] for node in nodes]
                for corner in range(8):
                    if corner < 4:
                        held[corner] = held[corner] + terms[corner]
                    else:
                        held[corner] = held[corner] - terms[7 - corner]
                for corner in range(8):
                    total[pl.ds(nodes[corner], 1), :] = held[corner]
            return carry

        lax.fori_loop(0, (live + SCATTER_UNROLL - 1) // SCATTER_UNROLL, scatter, 0)

    devices = reply_ref.shape[0]
    for position in range(LANES // SLOTS):
        values = reply_ref[...]
        if position:
            values = pltpu.roll(values, LANES - position * SLOTS, 1)
        reply_rows[position * devices : (position + 1) * devices, :] = values
    first = jnp.where(lane < 3, PENALTY, 0.0)

    def layer(chunk, carry):
        base = chunk * LAYER_UNROLL
        steps = range(LAYER_UNROLL)
        nodes = [layer_ref[0, base + step] for step in steps]
        held = [total[pl.ds(node, 1), :] for node in nodes]
        for step in steps:
            reply = reply_rows[pl.ds(slot_ref[0, base + step], 1), :]
            held[step] = held[step] + (reply - layer_rows[pl.ds(base + step, 1), :]) * first
        for step in steps:
            total[pl.ds(nodes[step], 1), :] = held[step]
        return carry

    lax.fori_loop(0, layers // LAYER_UNROLL, layer, 0)

    def fold(part, carry):
        for tile in range(own // LANES):
            start = aligned(part * own + tile * LANES)
            block = total[pl.ds(start, LANES), 0:SLOTS].T
            out_ref[part, :, tile * LANES : (tile + 1) * LANES] = (
                block[0:3] + block[3:6] + block[6:9]
            )
        return carry

    lax.fori_loop(0, owners, fold, 0)


def box_forces(layer_ids, slot_index, ids, disp, params, replies):
    owners, _, own = disp.shape
    slots = params.shape[1] * LANES // 3 * owners
    layers = layer_ids.shape[1]
    smem = pl.BlockSpec(memory_space=pltpu.SMEM)
    vmem = pl.BlockSpec(memory_space=pltpu.VMEM)
    f32, i32 = jnp.float32, jnp.int32
    return pl.pallas_call(
        box_kernel,
        out_shape=jax.ShapeDtypeStruct((owners, 3, own), f32),
        in_specs=[smem, smem, pl.BlockSpec(memory_space=pl.ANY), vmem, vmem, vmem],
        out_specs=vmem,
        scratch_shapes=[
            pltpu.VMEM((owners * own, LANES), f32),
            pltpu.VMEM((slots, LANES), f32),
            pltpu.VMEM((layers, LANES), f32),
            pltpu.VMEM((replies.shape[0] * (LANES // SLOTS), LANES), f32),
            pltpu.SMEM((owners * 1024,), i32),
        ]
        + [pltpu.SMEM((slots,), i32)] * 8
        + [pltpu.SemaphoreType.DMA((owners, 8)), pltpu.SemaphoreType.DMA((owners,))],
        compiler_params=pltpu.CompilerParams(vmem_limit_bytes=VMEM_LIMIT),
        name="box_forces",
    )(layer_ids, slot_index, ids, disp, params, replies)


def tiled_rows(field):
    lead, (rows, cols) = field.shape[:-2], field.shape[-2:]
    tiles = field.reshape(lead + (rows // 8, 8, cols // LANES, LANES))
    tiles = jnp.swapaxes(tiles, -3, -2)
    return tiles.reshape(lead[:-1] + (-1, LANES))


def untiled_rows(values, shape):
    rows, cols = shape[-2:]
    tiles = values.reshape(shape[:-2] + (rows // 8, cols // LANES, 8, LANES))
    return jnp.swapaxes(tiles, -3, -2).reshape(shape)


def on_device(
    grid_now,
    grid_before,
    wave_factor,
    layer_owner,
    layer_cell,
    box_now,
    box_before,
    node_mass,
    corner_nodes,
    live_counts,
    shear_modulus,
    lame_lambda,
    strain_scale,
    layer_nodes,
):
    count_x, count_y = lax.axis_size("gx"), lax.axis_size("gy")
    devices = count_x * count_y
    own_disp = box_now.reshape(3, -1)

    owners = layer_owner.reshape(-1)
    cell_index = layer_cell.reshape(-1)
    capacity = 2 * owners.shape[0] // devices
    rank_rows = jnp.arange(owners.shape[0])
    earlier = (rank_rows[None, :] < rank_rows[:, None]).astype(jnp.bfloat16)
    matches = owners[:, None] == jnp.arange(devices)[None, :]
    before = jnp.dot(earlier, matches.astype(jnp.bfloat16), preferred_element_type=jnp.float32)
    position = jnp.sum(jnp.where(matches, before, 0.0), axis=1).astype(jnp.int32)
    request = (
        jnp.zeros((devices * capacity,), jnp.int32)
        .at[owners * capacity + position]
        .set(cell_index, unique_indices=True)
    )
    request = jnp.pad(request.reshape(devices, capacity), ((0, 0), (0, LANES - capacity)))
    slot_index = position * devices + owners

    slots = corner_nodes.shape[2]
    tiles = slots // LANES // count_y
    ids = corner_nodes.reshape(8, tiles, count_y, LANES)
    ids = jnp.transpose(ids, (2, 0, 1, 3)).reshape(count_y, 8 * tiles, LANES)
    count_rows = jnp.broadcast_to(live_counts.reshape(1, 1, 1), (count_y, 8, LANES))
    ids = jnp.concatenate([ids, count_rows], axis=1)
    params = jnp.stack([shear_modulus, lame_lambda, strain_scale])
    params = params.reshape(3, tiles, count_y, LANES)
    params = jnp.transpose(params, (2, 0, 1, 3)).reshape(count_y, 3 * tiles, LANES)

    after, all_disp, all_ids, all_params, replies = grid_steps(
        tiled_rows(grid_now),
        tiled_rows(grid_before),
        tiled_rows(wave_factor),
        request.reshape(count_x, count_y, LANES),
        own_disp,
        ids,
        params,
        count_x,
        count_y,
    )
    node_term = box_forces(
        layer_nodes,
        slot_index.reshape(1, -1),
        all_ids.reshape(-1),
        all_disp,
        all_params,
        replies.reshape(devices, LANES),
    )
    parts = lax.all_to_all(node_term, "gy", split_axis=0, concat_axis=0, tiled=True)
    summed = jnp.sum(parts, axis=0)
    box_after = 2.0 * own_disp - box_before.reshape(3, -1) + STEP_SQUARE / node_mass * summed
    return (untiled_rows(after, grid_now.shape), box_after.reshape(box_now.shape))


def solution(mesh):
    return jax.shard_map(
        on_device,
        mesh=mesh,
        in_specs=(
            P(None, "gx", "gy", None),
            P(None, "gx", "gy", None),
            P("gx", "gy", None),
            P("gx", "gy", None),
            P("gx", "gy"),
            P(None, "gx", "gy"),
            P(None, "gx", "gy"),
            P("gx", "gy"),
            P(None, "gx", "gy"),
            P("gx", "gy"),
            P("gx", "gy"),
            P("gx", "gy"),
            P("gx", "gy"),
            P("gx", "gy"),
        ),
        out_specs=(P(None, "gx", "gy", None), P(None, "gx", "gy")),
        check_vma=False,
    )
```

time: 1390 us -> 236 us (0.17)
  other arithmetic: 584 us -> 3.77 us
  local copies, waits for them, and re-layouts: 382 us -> 13.1 us
  Pallas kernels: 0 us -> 195 us
  waiting for transfers between devices: 189 us -> 16.8 us
  blocking collectives: 156 us -> 0 us
  starting transfers between devices: 55.8 us -> 3.58 us
  between operations: 15.8 us -> 1.4 us
    scatter-add x9 -> x0, other arithmetic: 534 us -> none  [the longest x8 503 us: on_device(): node_term.at[:, corner_ids[corner]]]
    gather x2 -> x0, local copies, waits for them, and re-layouts: 252 us -> none  [the longest x1 227 us: on_device(): jnp.take(all_disp, corner_ids.reshape(-1), axis=1, mode='clip')]
    pallas_call x0 -> x2, Pallas kernels: none -> 195 us  [the longest x1 145 us: box_forces(): pl.pallas_call(box_kernel, out_shape=jax.ShapeDtypeStruct((owners, 3, own...]
    unnamed x2 -> x0, waiting for transfers between devices: 181 us -> none
    all_gather x1 -> x0, blocking collectives: 156 us -> none  [on_device(): all_disp = lax.all_gather(own_disp, 'gy', axis=1, tiled=True)]
    add x1 -> x0, local copies, waits for them, and re-layouts: 63.8 us -> none  [advance(): 2.0 * current - previous]
    all_to_all x2 -> x1, starting transfers between devices: 33 us -> 3.58 us  [on_device(): lax.all_to_all(node_term, 'gy', split_axis=0, concat_axis=0, tiled=True)]
    ppermute x8 -> x0, starting transfers between devices: 22.5 us -> none  [the longest x4 15.1 us: extended_2(): lax.ppermute(lax.slice_in_dim(block, block.shape[dim] - width, None, axis...]
  transfers between devices with their start and end apart: 11 -> 1, of which waited for: 3 -> 1; matrix products, arithmetic and copies ran while one was open for 59% -> 0% of each run, Pallas kernels for 0% -> 0%
where the time goes in v2:
time: 236 us; the launch traced here: 235 us
  Pallas kernels  195 us (83%)
  waiting for transfers between devices  16.8 us (7%)
  local copies, waits for them, and re-layouts  13.1 us (6%)
  other arithmetic  3.77 us (2%)
  starting transfers between devices  3.58 us (2%)
    pallas_call x1, Pallas kernels, box_forces(): pl.pallas_call(box_kernel, out_shape=jax.ShapeDtypeStruct((owners, 3, own...  145 us
    pallas_call x1, Pallas kernels, grid_steps(): pl.pallas_call(grid_kernel, out_shape=(jax.ShapeDtypeStruct(now.shape, f3...  50.5 us
    all_to_all x1, waiting for transfers between devices, on_device(): lax.all_to_all(node_term, 'gy', split_axis=0, concat_axis=0, tiled=True)  16.8 us
    unnamed x8, local copies, waits for them, and re-layouts  5.71 us
  transfers between devices with their start and end apart: 1, of which 1 were waited for; matrix products, arithmetic and copies ran while one was open for 0% of the time, Pallas kernels for 0%

profile of v2, /device:TPU:4, one launch (start us, length us, event | category | flops | bytes accessed | tf_op | source)
XLA Modules:
  0.0 234.9 jit_solution(12597602887457155771)
XLA Ops:
  0.6 1.1 fusion
  1.7 0.7 compare_select_fusion
  2.4 2.6 %scatter_custom_fusion = s32[1024]{0:T(1024)S(1)} fusion(s32[512]{0:T(512)S(1)} %bitcast.68, s32[512]{0:T(512)} %bitcast.69, s32[]{:T(128)} %constant.7.clone.1), kind=kCustom, calls=%fused_computation.15 | custom fusion | bytes 4608 | tf_op jit(solution)/shard_map/scatter | solution.py:628
  5.0 0.1 reshape.164
  5.1 0.6 pad_bitcast_fusion.request
  5.7 1.0 copy.27
  7.4 0.8 copy.21
  8.2 0.8 copy.22
  8.9 0.8 copy.23
  9.7 1.6 copy.28
  11.3 1.3 bitcast_add_fusion.slot_ref
  12.6 0.7 concatenate.4.ids_hbm
  13.3 0.6 maximum_bitcast_fusion.params_hbm
  13.9 50.5 %grid_steps.1 = (f32[3,2048,128]{2,1,0:T(8,128)}, f32[8,3,8960]{2,1,0:T(4,128)}, s32[8,72,128]{2,1,0:T(8,128)}, f32[8,24,128]{2,1,0:T(8,128)}, f32[16,8,128]{2,1,0:T(8,128)}) custom-call(f32[3,2048,128]{2,1,0:T(8,128)} %bitcast.53, f32[3,2048,128]{2,1,0:T(8,128)} %bitcast.54, f32[2048,128]{1,0:T(8,128)} %bitcast.56, s32[16,8,128]{2,1,0:T(8,128)} %pad_bitcast_fusion.request, ...), custom_call_target="tpu_custom_call" | custom-call | tf_op jit(solution)/shard_map/grid_steps/pallas_call | solution.py:329
  64.4 0.0 copy-start.2
  64.5 0.0 copy-start
  64.5 0.0 copy-start.1
  64.5 144.7 %box_forces.1 = f32[8,3,8960]{2,1,0:T(4,128)} custom-call(s32[1,512]{1,0:T(1,128)} %layer_ref.1, s32[1,512]{1,0:T(1,128)} %bitcast_add_fusion.slot_ref, s32[73728]{0:T(1024)} %bitcast.59, f32[8,3,8960]{2,1,0:T(4,128)} %get-tuple-element.9.disp_ref, f32[8,24,128]{2,1,0:T(8,128)} %get-tuple-element.10.params_ref, f32[128,128]{1,0:T(8,128)} %bitcast.61), custom_call_target="tpu_custom_call" | custom-call | tf_op jit(solution)/shard_map/box_forces/pallas_call | solution.py:565
  209.2 3.6 %all-to-all-start = ((f32[8,3,8960]{2,1,0:T(4,128)}), f32[8,3,8960]{2,1,0:T(4,128)S(1)}, u32[]{:S(2)}, u32[]{:S(2)}) async-start(f32[8,3,8960]{2,1,0:T(4,128)} %box_forces.1), calls=%async_computation | async-start | bytes 2293760 | tf_op jit(solution)/shard_map/all_to_all | solution.py:662
  212.8 0.0 copy-done.2
  212.8 0.1 divide_reduce_fusion
  212.9 16.8 %all-to-all-done = f32[8,3,8960]{2,1,0:T(4,128)S(1)} async-done(((f32[8,3,8960]{2,1,0:T(4,128)}), f32[8,3,8960]{2,1,0:T(4,128)S(1)}, u32[]{:S(2)}, u32[]{:S(2)}) %all-to-all-start) | async-done | bytes 860192 | tf_op jit(solution)/shard_map/all_to_all | solution.py:662
  229.7 0.2 reduce_sum.21
  229.9 0.0 copy-done
  229.9 0.0 copy-done.1
  230.0 0.8 multiply_add_fusion
  230.8 4.1 %copy.31 = f32[3,16,32,512]{3,2,1,0:T(8,128)} copy(f32[3,16,32,512]{3,2,1,0:T(8,128)} %bitcast.55) | data formatting | bytes 6291456
  (2 shorter events, 0.0 us)
Async XLA Ops:
  64.4 148.3 %copy-start.2 = (f32[1,8960]{1,0:T(1,128)S(1)}, f32[1,8960]{1,0:T(1,128)}, u32[]{:S(2)}) copy-start(f32[1,8960]{1,0:T(1,128)} %param.21) | copy-start | bytes 107524
  64.5 165.5 %copy-start = (f32[3,1,8960]{2,1,0:T(1,128)S(1)}, f32[3,1,8960]{2,1,0:T(1,128)}, u32[]{:S(2)}) copy-start(f32[3,1,8960]{2,1,0:T(1,128)} %param.19) | copy-start | bytes 322564
  64.5 165.5 %copy-start.1 = (f32[3,1,8960]{2,1,0:T(1,128)S(1)}, f32[3,1,8960]{2,1,0:T(1,128)}, u32[]{:S(2)}) copy-start(f32[3,1,8960]{2,1,0:T(1,128)} %param.20) | copy-start | bytes 322564
  209.2 20.5 %all-to-all-start = ((f32[8,3,8960]{2,1,0:T(4,128)}), f32[8,3,8960]{2,1,0:T(4,128)S(1)}, u32[]{:S(2)}, u32[]{:S(2)}) async-start(f32[8,3,8960]{2,1,0:T(4,128)} %box_forces.1), calls=%async_computation | async-start | bytes 2293760 | tf_op jit(solution)/shard_map/all_to_all | solution.py:662

commit v3 on v2

--- a/solution.py
+++ b/solution.py
@@ -15,8 +15,9 @@
 PLANE = 128
 VMEM_LIMIT = 58 * 2**20
 GATHER_UNROLL = 16
-SCATTER_UNROLL = 2
+SCATTER_UNROLL = 8
 LAYER_UNROLL = 16
+GROUP = 8
 MESH = pl.DeviceIdType.MESH
 
 
@@ -212,12 +213,12 @@
     for step in range(1, count_y):
         peer = lax.rem(gy + step, count_y)
         bulk.append(send(disp_hbm, disp_all.at[gy], (gx, peer)))
-        bulk.append(send(ids_hbm.at[peer], ids_all.at[gy], (gx, peer)))
-        bulk.append(send(params_hbm.at[peer], params_all.at[gy], (gx, peer)))
+        bulk.append(send(ids_hbm.at[step], ids_all.at[gy], (gx, peer)))
+        bulk.append(send(params_hbm.at[step], params_all.at[gy], (gx, peer)))
     own = [
         pltpu.make_async_copy(disp_hbm, disp_all.at[gy], local_sems.at[3]),
-        pltpu.make_async_copy(ids_hbm.at[gy], ids_all.at[gy], local_sems.at[4]),
-        pltpu.make_async_copy(params_hbm.at[gy], params_all.at[gy], local_sems.at[5]),
+        pltpu.make_async_copy(ids_hbm.at[0], ids_all.at[gy], local_sems.at[4]),
+        pltpu.make_async_copy(params_hbm.at[0], params_all.at[gy], local_sems.at[5]),
     ]
     for copy in own:
         copy.start()
@@ -383,10 +384,10 @@
 
 
 def box_kernel(
-    layer_ref, slot_ref, ids_hbm, disp_ref, params_ref, reply_ref,
-    out_ref, table, rows, layer_rows, reply_rows, counts, *rest,
+    layer_ref, slot_ref, ids_hbm, disp_ref, params_ref, reply_ref, field_in,
+    out_ref, field_out, table, rows, layer_rows, reply_rows, field, counts, *rest,
 ):
-    ids, sems, count_sem = rest[:8], rest[8], rest[9]
+    ids, sems, count_sem, field_sem = rest[:8], rest[8], rest[9], rest[10]
     owners, _, own = disp_ref.shape
     stripe = ids[0].shape[0] // owners
     span = ID_ROWS * LANES
@@ -409,6 +410,8 @@
             )
     for copy in copies:
         copy.start()
+    field_load = pltpu.make_async_copy(field_in, field, field_sem.at[0])
+    field_load.start()
 
     def build(part, carry):
         for tile in range(own // LANES):
@@ -418,20 +421,24 @@
         return carry
 
     lax.fori_loop(0, owners, build, 0)
+    field_load.wait()
+    field_store = pltpu.make_async_copy(field, field_out, field_sem.at[1])
+    field_store.start()
     signs = [gradient_signs(corner) for corner in range(8)]
     mine = lax.axis_index("gy")
 
     def live_of(part):
         count = counts[part * 1024]
         whole = count // LANES
-        tiles = (whole + owners - 1 - mine) // owners
-        partial = jnp.where(whole % owners == mine, count % LANES, 0)
+        turn = lax.rem(mine - part + owners, owners)
+        tiles = (whole + owners - 1 - turn) // owners
+        partial = jnp.where(whole % owners == turn, count % LANES, 0)
         return tiles * LANES + partial
 
-    for copy in copies:
-        copy.wait()
 
     for part in range(owners):
+        for copy in copies[9 * part : 9 * part + 9]:
+            copy.wait()
 
         def gather(chunk, carry, part=part):
             base = part * stripe + chunk * GATHER_UNROLL
@@ -490,15 +497,24 @@
             index = tile * LANES + lane
 
             def signed(value):
-                return jnp.where(index < live, -value, 0.0)
+                return jnp.where(index < live, -0.25 * value, 0.0)
 
             p00 = signed(volume + softened * s00)
             p11 = signed(volume + softened * s11)
             p22 = signed(volume + softened * s22)
             p01, p02, p12 = signed(softened * s01), signed(softened * s02), signed(softened * s12)
-            rows[pl.ds(start, LANES), 0:SLOTS] = rows_of(
-                jnp.concatenate([p00, p01, p02, p01, p11, p12, p02, p12, p22], axis=0)
-            )
+            pad = jnp.zeros((GROUP - 3, LANES), jnp.float32)
+            sides = [
+                jnp.concatenate(column + [pad], axis=0)
+                for column in ([p00, p01, p02], [p01, p11, p12], [p02, p12, p22])
+            ]
+            ends = []
+            for corner in range(4):
+                term = sides[0] if corner & 1 else -sides[0]
+                term = term + sides[1] if corner & 2 else term - sides[1]
+                ends.append(term - sides[2])
+            ends += [-ends[7 - corner] for corner in range(4, 8)]
+            rows[pl.ds(start, LANES), 0 : 8 * GROUP] = jnp.concatenate(ends, axis=0).T
             return carry
 
         lax.fori_loop(0, (live + LANES - 1) // LANES, element, 0)
@@ -507,16 +523,9 @@
             base = part * stripe + chunk * SCATTER_UNROLL
             for step in range(SCATTER_UNROLL):
                 line = rows[pl.ds(base + step, 1), :]
-                nodes = [ids[corner][base + step] for corner in range(8)]
-                terms = [line * signs[corner] for corner in range(4)]
-                held = [total[pl.ds(node, 1), :] for node in nodes]
                 for corner in range(8):
-                    if corner < 4:
-                        held[corner] = held[corner] + terms[corner]
-                    else:
-                        held[corner] = held[corner] - terms[7 - corner]
-                for corner in range(8):
-                    total[pl.ds(nodes[corner], 1), :] = held[corner]
+                    own_lanes = slice(corner * GROUP, (corner + 1) * GROUP)
+                    total[pl.ds(ids[corner][base + step], 1), own_lanes] = line[:, own_lanes]
             return carry
 
         lax.fori_loop(0, (live + SCATTER_UNROLL - 1) // SCATTER_UNROLL, scatter, 0)
@@ -527,7 +536,7 @@
         if position:
             values = pltpu.roll(values, LANES - position * SLOTS, 1)
         reply_rows[position * devices : (position + 1) * devices, :] = values
-    first = jnp.where(lane < 3, PENALTY, 0.0)
+    inside = lane < 3
 
     def layer(chunk, carry):
         base = chunk * LAYER_UNROLL
@@ -536,7 +545,8 @@
         held = [total[pl.ds(node, 1), :] for node in nodes]
         for step in steps:
             reply = reply_rows[pl.ds(slot_ref[0, base + step], 1), :]
-            held[step] = held[step] + (reply - layer_rows[pl.ds(base + step, 1), :]) * first
+            gap = reply - layer_rows[pl.ds(base + step, 1), :]
+            held[step] = held[step] + jnp.where(inside, PENALTY * gap, 0.0)
         for step in steps:
             total[pl.ds(nodes[step], 1), :] = held[step]
         return carry
@@ -546,39 +556,50 @@
     def fold(part, carry):
         for tile in range(own // LANES):
             start = aligned(part * own + tile * LANES)
-            block = total[pl.ds(start, LANES), 0:SLOTS].T
-            out_ref[part, :, tile * LANES : (tile + 1) * LANES] = (
-                block[0:3] + block[3:6] + block[6:9]
-            )
+            block = total[pl.ds(start, LANES), 0 : 8 * GROUP].T
+            terms = [block[corner * GROUP : corner * GROUP + GROUP] for corner in range(8)]
+            while len(terms) > 1:
+                terms = [a + b for a, b in zip(terms[0::2], terms[1::2])]
+            out_ref[part, :, tile * LANES : (tile + 1) * LANES] = terms[0][0:3]
         return carry
 
     lax.fori_loop(0, owners, fold, 0)
-
-
-def box_forces(layer_ids, slot_index, ids, disp, params, replies):
+    field_store.wait()
+
+
+def box_forces(layer_ids, slot_index, ids, disp, params, replies, field):
     owners, _, own = disp.shape
     slots = params.shape[1] * LANES // 3 * owners
     layers = layer_ids.shape[1]
     smem = pl.BlockSpec(memory_space=pltpu.SMEM)
     vmem = pl.BlockSpec(memory_space=pltpu.VMEM)
+    hbm = pl.BlockSpec(memory_space=pl.ANY)
     f32, i32 = jnp.float32, jnp.int32
     return pl.pallas_call(
         box_kernel,
-        out_shape=jax.ShapeDtypeStruct((owners, 3, own), f32),
-        in_specs=[smem, smem, pl.BlockSpec(memory_space=pl.ANY), vmem, vmem, vmem],
-        out_specs=vmem,
+        out_shape=(
+            jax.ShapeDtypeStruct((owners, 3, own), f32),
+            jax.ShapeDtypeStruct(field.shape, f32),
+        ),
+        in_specs=[smem, smem, hbm, vmem, vmem, vmem, hbm],
+        out_specs=(vmem, hbm),
         scratch_shapes=[
             pltpu.VMEM((owners * own, LANES), f32),
             pltpu.VMEM((slots, LANES), f32),
             pltpu.VMEM((layers, LANES), f32),
             pltpu.VMEM((replies.shape[0] * (LANES // SLOTS), LANES), f32),
+            pltpu.VMEM(field.shape, f32),
             pltpu.SMEM((owners * 1024,), i32),
         ]
         + [pltpu.SMEM((slots,), i32)] * 8
-        + [pltpu.SemaphoreType.DMA((owners, 8)), pltpu.SemaphoreType.DMA((owners,))],
+        + [
+            pltpu.SemaphoreType.DMA((owners, 8)),
+            pltpu.SemaphoreType.DMA((owners,)),
+            pltpu.SemaphoreType.DMA((2,)),
+        ],
         compiler_params=pltpu.CompilerParams(vmem_limit_bytes=VMEM_LIMIT),
         name="box_forces",
-    )(layer_ids, slot_index, ids, disp, params, replies)
+    )(layer_ids, slot_index, ids, disp, params, replies, field)
 
 
 def tiled_rows(field):
@@ -651,13 +672,14 @@
         count_x,
         count_y,
     )
-    node_term = box_forces(
+    node_term, after = box_forces(
         layer_nodes,
         slot_index.reshape(1, -1),
         all_ids.reshape(-1),
         all_disp,
         all_params,
         replies.reshape(devices, LANES),
+        after,
     )
     parts = lax.all_to_all(node_term, "gy", split_axis=0, concat_axis=0, tiled=True)
     summed = jnp.sum(parts, axis=0)

time: 236 us -> 181 us (0.77)
  Pallas kernels: 195 us -> 142 us
  local copies, waits for them, and re-layouts: 13.1 us -> 8.94 us
    pallas_call x1, Pallas kernels: 145 us -> 91.7 us  [box_forces(): pl.pallas_call(box_kernel, out_shape=(jax.ShapeDtypeStruct((owners, 3, ow...]
    unnamed x8 -> x7, local copies, waits for them, and re-layouts: 5.71 us -> 1.6 us
where the time goes in v3:
time: 181 us; the launch traced here: 179 us
  Pallas kernels  142 us (78%)
  waiting for transfers between devices  16.9 us (9%)
  local copies, waits for them, and re-layouts  8.94 us (5%)
  starting transfers between devices  4.51 us (2%)
  other arithmetic  3.78 us (2%)
    pallas_call x1, Pallas kernels, box_forces(): pl.pallas_call(box_kernel, out_shape=(jax.ShapeDtypeStruct((owners, 3, ow...  91.7 us
    pallas_call x1, Pallas kernels, grid_steps(): pl.pallas_call(grid_kernel, out_shape=(jax.ShapeDtypeStruct(now.shape, f3...  50.5 us
    all_to_all x1, waiting for transfers between devices, on_device(): lax.all_to_all(node_term, 'gy', split_axis=0, concat_axis=0, tiled=True)  16.9 us
    all_to_all x1, starting transfers between devices, on_device(): lax.all_to_all(node_term, 'gy', split_axis=0, concat_axis=0, tiled=True)  4.51 us
  transfers between devices with their start and end apart: 1, of which 1 were waited for; matrix products, arithmetic and copies ran while one was open for 0% of the time, Pallas kernels for 0%

profile of v3, /device:TPU:4, one launch (start us, length us, event | category | flops | bytes accessed | tf_op | source)
XLA Modules:
  0.0 178.8 jit_solution(3986613384030185860)
XLA Ops:
  0.6 1.1 fusion
  1.7 0.7 compare_select_fusion
  2.4 2.6 %scatter_custom_fusion = s32[1024]{0:T(1024)S(1)} fusion(s32[512]{0:T(512)S(1)} %bitcast.67, s32[512]{0:T(512)} %bitcast.69, s32[]{:T(128)} %constant.0.clone.1), kind=kCustom, calls=%fused_computation.15 | custom fusion | bytes 4608 | tf_op jit(solution)/shard_map/scatter | solution.py:649
  5.0 0.1 reshape.165
  5.1 0.6 pad_bitcast_fusion.request
  5.7 1.0 copy.27
  7.4 0.8 copy.21
  8.2 0.8 copy.22
  8.9 0.8 copy.23
  9.7 1.6 copy.28
  11.3 1.3 bitcast_add_fusion.1.slot_ref
  12.5 0.7 concatenate.4.ids_hbm
  13.3 0.6 maximum_bitcast_fusion.params_hbm
  13.9 50.5 %grid_steps.1 = (f32[3,2048,128]{2,1,0:T(8,128)}, f32[8,3,8960]{2,1,0:T(4,128)}, s32[8,72,128]{2,1,0:T(8,128)}, f32[8,24,128]{2,1,0:T(8,128)}, f32[16,8,128]{2,1,0:T(8,128)}) custom-call(f32[3,2048,128]{2,1,0:T(8,128)} %bitcast.53, f32[3,2048,128]{2,1,0:T(8,128)} %bitcast.54, f32[2048,128]{1,0:T(8,128)} %bitcast.55, s32[16,8,128]{2,1,0:T(8,128)} %pad_bitcast_fusion.request, ...), custom_call_target="tpu_custom_call" | custom-call | tf_op jit(solution)/shard_map/grid_steps/pallas_call | solution.py:330
  64.4 0.0 copy-start.2
  64.4 0.0 copy-start
  64.5 0.0 copy-start.1
  64.5 91.7 %box_forces.1 = (f32[8,3,8960]{2,1,0:T(4,128)}, f32[3,2048,128]{2,1,0:T(8,128)}) custom-call(s32[1,512]{1,0:T(1,128)} %layer_ref.1, s32[1,512]{1,0:T(1,128)} %bitcast_add_fusion.1.slot_ref, s32[73728]{0:T(1024)} %bitcast.58, f32[8,3,8960]{2,1,0:T(4,128)} %get-tuple-element.10.disp_ref, f32[8,24,128]{2,1,0:T(8,128)} %get-tuple-element.11.params_ref, ...), custom_call_target="tpu_custom_call" | custom-call | tf_op jit(solution)/shard_map/box_forces/pallas_call | solution.py:578
  156.2 4.5 %all-to-all-start = ((f32[8,3,8960]{2,1,0:T(4,128)}), f32[8,3,8960]{2,1,0:T(4,128)S(1)}, u32[]{:S(2)}, u32[]{:S(2)}) async-start(f32[8,3,8960]{2,1,0:T(4,128)} %get-tuple-element.15), calls=%async_computation | async-start | bytes 2293760 | tf_op jit(solution)/shard_map/all_to_all | solution.py:684
  160.7 0.0 copy-done.2
  160.7 0.1 divide_reduce_fusion
  160.9 16.9 %all-to-all-done = f32[8,3,8960]{2,1,0:T(4,128)S(1)} async-done(((f32[8,3,8960]{2,1,0:T(4,128)}), f32[8,3,8960]{2,1,0:T(4,128)S(1)}, u32[]{:S(2)}, u32[]{:S(2)}) %all-to-all-start) | async-done | bytes 860192 | tf_op jit(solution)/shard_map/all_to_all | solution.py:684
  177.8 0.2 reduce_sum.21
  178.0 0.0 copy-done
  178.0 0.0 copy-done.1
  178.0 0.8 multiply_add_fusion
  (2 shorter events, 0.0 us)
Async XLA Ops:
  64.4 96.3 %copy-start.2 = (f32[1,8960]{1,0:T(1,128)S(1)}, f32[1,8960]{1,0:T(1,128)}, u32[]{:S(2)}) copy-start(f32[1,8960]{1,0:T(1,128)} %param.21) | copy-start | bytes 107524
  64.4 113.5 %copy-start = (f32[3,1,8960]{2,1,0:T(1,128)S(1)}, f32[3,1,8960]{2,1,0:T(1,128)}, u32[]{:S(2)}) copy-start(f32[3,1,8960]{2,1,0:T(1,128)} %param.19) | copy-start | bytes 322564
  64.5 113.5 %copy-start.1 = (f32[3,1,8960]{2,1,0:T(1,128)S(1)}, f32[3,1,8960]{2,1,0:T(1,128)}, u32[]{:S(2)}) copy-start(f32[3,1,8960]{2,1,0:T(1,128)} %param.20) | copy-start | bytes 322564
  156.2 21.5 %all-to-all-start = ((f32[8,3,8960]{2,1,0:T(4,128)}), f32[8,3,8960]{2,1,0:T(4,128)S(1)}, u32[]{:S(2)}, u32[]{:S(2)}) async-start(f32[8,3,8960]{2,1,0:T(4,128)} %get-tuple-element.15), calls=%async_computation | async-start | bytes 2293760 | tf_op jit(solution)/shard_map/all_to_all | solution.py:684

commit v4 on v3

--- a/solution.py
+++ b/solution.py
@@ -23,6 +23,44 @@
 
 def aligned(start, unit=LANES):
     return pl.multiple_of(start, unit)
+
+
+def rank_kernel(owner_ref, cell_ref, request_out, slot_out):
+    devices, layers = request_out.shape[0], owner_ref.shape[1]
+    row = lax.broadcasted_iota(jnp.int32, (devices, layers), 0)
+    owner, cell = owner_ref[...], cell_ref[...]
+    found = row == owner
+    matches = jnp.where(found, 1.0, 0.0).astype(jnp.bfloat16)
+    first = lax.broadcasted_iota(jnp.int32, (layers, layers), 0)
+    second = lax.broadcasted_iota(jnp.int32, (layers, layers), 1)
+    earlier = jnp.where(first < second, 1.0, 0.0).astype(jnp.bfloat16)
+    before = jnp.dot(matches, earlier, preferred_element_type=jnp.float32)
+    position = jnp.sum(jnp.where(found, before, 0.0), axis=0, keepdims=True).astype(jnp.int32)
+    placed = row == position
+    request = jnp.zeros((devices, devices), jnp.int32)
+    for shift in (0, 6, 12):
+        digit = ((cell >> shift) & 63).astype(jnp.float32)
+        digits = jnp.where(placed, digit, 0.0).astype(jnp.bfloat16)
+        part = lax.dot_general(
+            matches, digits, (((1,), (1,)), ((), ())), preferred_element_type=jnp.float32
+        )
+        request = request + (part.astype(jnp.int32) << shift)
+    request_out[...] = request
+    slot_out[...] = position * devices + owner
+
+
+def rank_requests(owners, cells, devices):
+    vmem = pl.BlockSpec(memory_space=pltpu.VMEM)
+    return pl.pallas_call(
+        rank_kernel,
+        out_shape=(
+            jax.ShapeDtypeStruct((devices, LANES), jnp.int32),
+            jax.ShapeDtypeStruct(owners.shape, jnp.int32),
+        ),
+        in_specs=[vmem, vmem],
+        out_specs=(vmem, vmem),
+        name="rank_requests",
+    )(owners, cells)
 
 
 def wave_plane(comp, index, now, before, factor, out, out_shift):
@@ -106,10 +144,10 @@
 
 
 def grid_kernel(
-    now_hbm, before_hbm, factor_hbm, request, disp_hbm, ids_hbm, params_hbm,
+    now_hbm, before_hbm, factor_hbm, request, disp_raw, ids_raw, shear_raw, lame_raw, scale_raw, live,
     after_hbm, disp_all, ids_all, params_all, reply_out,
     now, mid, after, before, factor, y_sent, y_got, asked_x, asked_t, asked_y, rows_vmem,
-    rows_smem, found, found_x, found_t, send_sems, recv_sems, local_sems,
+    rows_smem, found, found_x, found_t, disp_own, ids_own, params_own, send_sems, recv_sems, local_sems,
 ):
     gx, gy = lax.axis_index("gx"), lax.axis_index("gy")
     count_x, count_y = lax.axis_size("gx"), lax.axis_size("gy")
@@ -209,16 +247,29 @@
     loads[0].wait()
     edges(0, now)
     first_y = y_halo(0)
+    for comp in range(3):
+        for tile in range(disp_raw.shape[1]):
+            disp_own[comp : comp + 1, tile * LANES : (tile + 1) * LANES] = disp_raw[comp, tile]
+    stripes = ids_raw.shape[1] // count_y
+    for turn in range(count_y):
+        every = pl.ds(turn, stripes, stride=count_y)
+        for corner in range(8):
+            here = slice(corner * stripes, (corner + 1) * stripes)
+            ids_own[turn, here, :] = ids_raw[corner, every, :]
+        ids_own[turn, 8 * stripes :, :] = jnp.full((8, LANES), live[0, 0], jnp.int32)
+        for index, raw in enumerate((shear_raw, lame_raw, scale_raw)):
+            here = slice(index * stripes, (index + 1) * stripes)
+            params_own[turn, here, :] = raw[every, :]
     bulk = []
     for step in range(1, count_y):
         peer = lax.rem(gy + step, count_y)
-        bulk.append(send(disp_hbm, disp_all.at[gy], (gx, peer)))
-        bulk.append(send(ids_hbm.at[step], ids_all.at[gy], (gx, peer)))
-        bulk.append(send(params_hbm.at[step], params_all.at[gy], (gx, peer)))
+        bulk.append(send(disp_own, disp_all.at[gy], (gx, peer)))
+        bulk.append(send(ids_own.at[step], ids_all.at[gy], (gx, peer)))
+        bulk.append(send(params_own.at[step], params_all.at[gy], (gx, peer)))
     own = [
-        pltpu.make_async_copy(disp_hbm, disp_all.at[gy], local_sems.at[3]),
-        pltpu.make_async_copy(ids_hbm.at[0], ids_all.at[gy], local_sems.at[4]),
-        pltpu.make_async_copy(params_hbm.at[0], params_all.at[gy], local_sems.at[5]),
+        pltpu.make_async_copy(disp_own, disp_all.at[gy], local_sems.at[3]),
+        pltpu.make_async_copy(ids_own.at[0], ids_all.at[gy], local_sems.at[4]),
+        pltpu.make_async_copy(params_own.at[0], params_all.at[gy], local_sems.at[5]),
     ]
     for copy in own:
         copy.start()
@@ -319,7 +370,7 @@
     store.wait()
 
 
-def grid_steps(now, before, factor, request, disp, ids, params, count_x, count_y):
+def grid_steps(now, before, factor, request, disp, ids, params, live, count_x, count_y):
     rows = factor.shape[0]
     f32, i32 = jnp.float32, jnp.int32
     hbm = pl.BlockSpec(memory_space=pl.ANY)
@@ -327,16 +378,17 @@
     halo_rows = rows + 4 * PLANE
     copies = 8 + 3 * (count_y - 1) + 2 * (count_x - 1) + 2 * (count_y - 1)
     planes = rows // PLANE
+    stripes = ids.shape[1] // count_y
     return pl.pallas_call(
         grid_kernel,
         out_shape=(
             jax.ShapeDtypeStruct(now.shape, f32),
-            jax.ShapeDtypeStruct((count_y,) + disp.shape, f32),
-            jax.ShapeDtypeStruct(ids.shape, i32),
-            jax.ShapeDtypeStruct(params.shape, f32),
+            jax.ShapeDtypeStruct((count_y, 3, disp.shape[1] * LANES), f32),
+            jax.ShapeDtypeStruct((count_y, ID_ROWS, LANES), i32),
+            jax.ShapeDtypeStruct((count_y, 3 * stripes, LANES), f32),
             jax.ShapeDtypeStruct(request.shape, f32),
         ),
-        in_specs=[hbm, hbm, hbm, vmem, hbm, hbm, hbm],
+        in_specs=[hbm, hbm, hbm] + [vmem] * 6 + [pl.BlockSpec(memory_space=pltpu.SMEM)],
         out_specs=(hbm, hbm, hbm, hbm, vmem),
         scratch_shapes=[
             pltpu.VMEM((3, halo_rows, LANES), f32),
@@ -354,6 +406,9 @@
             pltpu.VMEM((count_y, count_x, LANES), f32),
             pltpu.VMEM((count_y, count_x, LANES), f32),
             pltpu.VMEM((count_x, count_y, LANES), f32),
+            pltpu.VMEM((3, disp.shape[1] * LANES), f32),
+            pltpu.VMEM((count_y, ID_ROWS, LANES), i32),
+            pltpu.VMEM((count_y, 3 * stripes, LANES), f32),
             pltpu.SemaphoreType.DMA((copies,)),
             pltpu.SemaphoreType.DMA((copies,)),
             pltpu.SemaphoreType.DMA((8,)),
@@ -362,7 +417,7 @@
             vmem_limit_bytes=VMEM_LIMIT, collective_id=1, has_side_effects=True
         ),
         name="grid_steps",
-    )(now, before, factor, request, disp, ids, params)
+    )(now, before, factor, request, disp, ids, *params, live)
 
 
 def gradient_signs(corner):
@@ -602,6 +657,58 @@
     )(layer_ids, slot_index, ids, disp, params, replies, field)
 
 
+def sum_kernel(parts_hbm, out_ref, got, send_sems, recv_sems, local_sem):
+    gx, gy = lax.axis_index("gx"), lax.axis_index("gy")
+    count = lax.axis_size("gy")
+    own = pltpu.make_async_copy(parts_hbm.at[gy], got.at[0], local_sem.at[0])
+    own.start()
+    barrier = pltpu.get_barrier_semaphore()
+    for step in range(1, count):
+        peer = lax.rem(gy + step, count)
+        pl.semaphore_signal(barrier, inc=1, device_id=(gx, peer), device_id_type=MESH)
+    pl.semaphore_wait(barrier, count - 1)
+    copies = []
+    for step in range(1, count):
+        peer = lax.rem(gy + step, count)
+        copy = pltpu.make_async_remote_copy(
+            src_ref=parts_hbm.at[peer],
+            dst_ref=got.at[step],
+            send_sem=send_sems.at[step],
+            recv_sem=recv_sems.at[step],
+            device_id=(gx, peer),
+            device_id_type=MESH,
+        )
+        copy.start()
+        copies.append(copy)
+    own.wait()
+    for copy in copies:
+        copy.wait()
+    terms = [got[step] for step in range(count)]
+    while len(terms) > 1:
+        terms = [a + b for a, b in zip(terms[0::2], terms[1::2])]
+    out_ref[...] = terms[0]
+
+
+def sum_forces(parts):
+    count, comps, own = parts.shape
+    return pl.pallas_call(
+        sum_kernel,
+        out_shape=jax.ShapeDtypeStruct((comps, own), jnp.float32),
+        in_specs=[pl.BlockSpec(memory_space=pl.ANY)],
+        out_specs=pl.BlockSpec(memory_space=pltpu.VMEM),
+        scratch_shapes=[
+            pltpu.VMEM(parts.shape, jnp.float32),
+            pltpu.SemaphoreType.DMA((count,)),
+            pltpu.SemaphoreType.DMA((count,)),
+            pltpu.SemaphoreType.DMA((1,)),
+        ],
+        compiler_params=pltpu.CompilerParams(
+            vmem_limit_bytes=VMEM_LIMIT, collective_id=2, has_side_effects=True
+        ),
+        name="sum_forces",
+    )(parts)
+
+
 def tiled_rows(field):
     lead, (rows, cols) = field.shape[:-2], field.shape[-2:]
     tiles = field.reshape(lead + (rows // 8, 8, cols // LANES, LANES))
@@ -635,54 +742,33 @@
     devices = count_x * count_y
     own_disp = box_now.reshape(3, -1)
 
-    owners = layer_owner.reshape(-1)
-    cell_index = layer_cell.reshape(-1)
-    capacity = 2 * owners.shape[0] // devices
-    rank_rows = jnp.arange(owners.shape[0])
-    earlier = (rank_rows[None, :] < rank_rows[:, None]).astype(jnp.bfloat16)
-    matches = owners[:, None] == jnp.arange(devices)[None, :]
-    before = jnp.dot(earlier, matches.astype(jnp.bfloat16), preferred_element_type=jnp.float32)
-    position = jnp.sum(jnp.where(matches, before, 0.0), axis=1).astype(jnp.int32)
-    request = (
-        jnp.zeros((devices * capacity,), jnp.int32)
-        .at[owners * capacity + position]
-        .set(cell_index, unique_indices=True)
+    request, slot_index = rank_requests(
+        layer_owner.reshape(1, -1), layer_cell.reshape(1, -1), devices
     )
-    request = jnp.pad(request.reshape(devices, capacity), ((0, 0), (0, LANES - capacity)))
-    slot_index = position * devices + owners
-
-    slots = corner_nodes.shape[2]
-    tiles = slots // LANES // count_y
-    ids = corner_nodes.reshape(8, tiles, count_y, LANES)
-    ids = jnp.transpose(ids, (2, 0, 1, 3)).reshape(count_y, 8 * tiles, LANES)
-    count_rows = jnp.broadcast_to(live_counts.reshape(1, 1, 1), (count_y, 8, LANES))
-    ids = jnp.concatenate([ids, count_rows], axis=1)
-    params = jnp.stack([shear_modulus, lame_lambda, strain_scale])
-    params = params.reshape(3, tiles, count_y, LANES)
-    params = jnp.transpose(params, (2, 0, 1, 3)).reshape(count_y, 3 * tiles, LANES)
+    lines = (-1, LANES)
 
     after, all_disp, all_ids, all_params, replies = grid_steps(
         tiled_rows(grid_now),
         tiled_rows(grid_before),
         tiled_rows(wave_factor),
         request.reshape(count_x, count_y, LANES),
-        own_disp,
-        ids,
-        params,
+        box_now.reshape(3, -1, 1, LANES),
+        corner_nodes.reshape(8, -1, LANES),
+        [values.reshape(lines) for values in (shear_modulus, lame_lambda, strain_scale)],
+        live_counts,
         count_x,
         count_y,
     )
     node_term, after = box_forces(
         layer_nodes,
-        slot_index.reshape(1, -1),
+        slot_index,
         all_ids.reshape(-1),
         all_disp,
         all_params,
         replies.reshape(devices, LANES),
         after,
     )
-    parts = lax.all_to_all(node_term, "gy", split_axis=0, concat_axis=0, tiled=True)
-    summed = jnp.sum(parts, axis=0)
+    summed = sum_forces(node_term)
     box_after = 2.0 * own_disp - box_before.reshape(3, -1) + STEP_SQUARE / node_mass * summed
     return (untiled_rows(after, grid_now.shape), box_after.reshape(box_now.shape))
 

time: 181 us -> 182 us (level)
  the two profiles are of different devices: /device:TPU:4 before, /device:TPU:67 now
where the time goes in v4:
time: 182 us
  Pallas kernels  178 us (98%)
    pallas_call x1, Pallas kernels, box_forces(): pl.pallas_call(box_kernel, out_shape=(jax.ShapeDtypeStruct((owners, 3, ow...  106 us
    pallas_call x1, Pallas kernels, grid_steps(): pl.pallas_call(grid_kernel, out_shape=(jax.ShapeDtypeStruct(now.shape, f3...  49.3 us
    pallas_call x1, Pallas kernels, sum_forces(): pl.pallas_call(sum_kernel, out_shape=jax.ShapeDtypeStruct((comps, own), j...  21.2 us

profile of v4, /device:TPU:67, one launch (start us, length us, event | category | flops | bytes accessed | tf_op | source)
XLA Modules:
  0.0 181.6 jit_solution(4168566280640679076)
XLA Ops:
  0.6 1.9 %rank_requests.1 = (s32[128,128]{1,0:T(8,128)}, s32[1,512]{1,0:T(1,128)}) custom-call(s32[1,512]{1,0:T(1,128)} %bitcast.46, s32[1,512]{1,0:T(1,128)} %cell_ref.1), custom_call_target="tpu_custom_call" | custom-call | tf_op jit(solution)/shard_map/rank_requests/pallas_call | solution.py:54
  3.2 49.3 %grid_steps.1 = (f32[3,2048,128]{2,1,0:T(8,128)}, f32[8,3,8960]{2,1,0:T(4,128)}, s32[8,72,128]{2,1,0:T(8,128)}, f32[8,24,128]{2,1,0:T(8,128)}, f32[16,8,128]{2,1,0:T(8,128)}) custom-call(f32[3,2048,128]{2,1,0:T(8,128)} %bitcast.35, f32[3,2048,128]{2,1,0:T(8,128)} %bitcast.36, f32[2048,128]{1,0:T(8,128)} %bitcast.37, s32[16,8,128]{2,1,0:T(8,128)} %bitcast.42, ...), custom_call_target="tpu_custom_call" | custom-call | tf_op jit(solution)/shard_map/grid_steps/pallas_call | solution.py:382
  52.5 0.0 copy-start.2
  52.5 0.0 copy-start
  52.5 0.0 copy-start.1
  52.5 106.0 %box_forces.1 = (f32[8,3,8960]{2,1,0:T(4,128)}, f32[3,2048,128]{2,1,0:T(8,128)}) custom-call(s32[1,512]{1,0:T(1,128)} %layer_ref.1, s32[1,512]{1,0:T(1,128)} %get-tuple-element.11.slot_ref, s32[73728]{0:T(1024)} %bitcast.39, f32[8,3,8960]{2,1,0:T(4,128)} %get-tuple-element.14.disp_ref, f32[8,24,128]{2,1,0:T(8,128)} %get-tuple-element.15.params_ref, ...), custom_call_target="tpu_custom_call" | custom-call | tf_op jit(solution)/shard_map/box_forces/pallas_call | solution.py:633
  158.6 21.2 %sum_forces.1 = f32[3,8960]{1,0:T(4,128)} custom-call(f32[8,3,8960]{2,1,0:T(4,128)} %get-tuple-element.19.parts_hbm), custom_call_target="tpu_custom_call" | custom-call | tf_op jit(solution)/shard_map/sum_forces/pallas_call | solution.py:694
  179.7 0.0 copy-done.2
  179.7 0.1 divide_reduce_fusion
  179.9 0.0 copy-done
  179.9 0.0 copy-done.1
  179.9 1.0 fusion
  180.9 0.8 copy.18
Async XLA Ops:
  52.5 127.3 %copy-start.2 = (f32[1,8960]{1,0:T(1,128)S(1)}, f32[1,8960]{1,0:T(1,128)}, u32[]{:S(2)}) copy-start(f32[1,8960]{1,0:T(1,128)} %param.21) | copy-start | bytes 107524
  52.5 127.4 %copy-start = (f32[3,1,8960]{2,1,0:T(1,128)S(1)}, f32[3,1,8960]{2,1,0:T(1,128)}, u32[]{:S(2)}) copy-start(f32[3,1,8960]{2,1,0:T(1,128)} %param.19) | copy-start | bytes 322564
  52.5 127.4 %copy-start.1 = (f32[3,1,8960]{2,1,0:T(1,128)S(1)}, f32[3,1,8960]{2,1,0:T(1,128)}, u32[]{:S(2)}) copy-start(f32[3,1,8960]{2,1,0:T(1,128)} %param.20) | copy-start | bytes 322564

commit v5 on v4

--- a/solution.py
+++ b/solution.py
@@ -14,8 +14,8 @@
 ID_ROWS = 72
 PLANE = 128
 VMEM_LIMIT = 58 * 2**20
-GATHER_UNROLL = 16
-SCATTER_UNROLL = 8
+GATHER_UNROLL = 32
+SCATTER_UNROLL = 16
 LAYER_UNROLL = 16
 GROUP = 8
 MESH = pl.DeviceIdType.MESH
@@ -148,6 +148,7 @@
     after_hbm, disp_all, ids_all, params_all, reply_out,
     now, mid, after, before, factor, y_sent, y_got, asked_x, asked_t, asked_y, rows_vmem,
     rows_smem, found, found_x, found_t, disp_own, ids_own, params_own, send_sems, recv_sems, local_sems,
+    store_sems,
 ):
     gx, gy = lax.axis_index("gx"), lax.axis_index("gy")
     count_x, count_y = lax.axis_size("gx"), lax.axis_size("gy")
@@ -192,61 +193,60 @@
     upper, lower = lax.rem(gy + 1, count_y), lax.rem(gy + count_y - 1, count_y)
     top = (planes - 2) * PLANE
 
-    def x_halo(source, shift, target):
+    def x_halo(source, shift, target, comp):
         return [
             send(
-                source.at[:, pl.ds(top + shift, edge), :],
-                target.at[:, pl.ds(0, edge), :],
+                source.at[comp, pl.ds(top + shift, edge), :],
+                target.at[comp, pl.ds(0, edge), :],
                 (right, gy),
             ),
             send(
-                source.at[:, pl.ds(shift, edge), :],
-                target.at[:, pl.ds(edge + planes * PLANE, edge), :],
+                source.at[comp, pl.ds(shift, edge), :],
+                target.at[comp, pl.ds(edge + planes * PLANE, edge), :],
                 (left, gy),
             ),
         ]
 
-    def y_halo(step):
+    def y_halo(step, comp):
         return [
-            send(y_sent.at[step, 1], y_got.at[step, 0], (gx, upper)),
-            send(y_sent.at[step, 0], y_got.at[step, 1], (gx, lower)),
+            send(y_sent.at[step, 1, comp], y_got.at[step, 0, comp], (gx, upper)),
+            send(y_sent.at[step, 0, comp], y_got.at[step, 1, comp], (gx, lower)),
         ]
 
-    def each_plane(indices, body):
-        def run(comp, carry):
-            for low, high in indices:
-                lax.fori_loop(low, high, lambda index, c: (body(comp, index), c)[1], 0)
-            return carry
-
-        lax.fori_loop(0, 3, run, 0)
-
-    def edges(step, source):
+    def each_plane(comp, ranges, body):
+        for low, high in ranges:
+            lax.fori_loop(low, high, lambda index, c: (body(comp, index), c)[1], 0)
+
+    def edges(step, source, comp):
         each_plane(
+            comp,
             [(0, planes)],
             lambda comp, index: y_edges(comp, index, source, y_sent.at[step, 0], y_sent.at[step, 1]),
         )
 
-    def clear_outside(target):
+    def clear_outside(target, comp):
         @pl.when(gx == 0)
         def _():
-            target[:, 0:edge, :] = jnp.zeros((3, edge, LANES), jnp.float32)
+            target[comp, 0:edge, :] = jnp.zeros((edge, LANES), jnp.float32)
 
         @pl.when(gx == count_x - 1)
         def _():
-            target[:, edge + planes * PLANE :, :] = jnp.zeros((3, edge, LANES), jnp.float32)
+            target[comp, edge + planes * PLANE :, :] = jnp.zeros((edge, LANES), jnp.float32)
 
     low_weight = jnp.where(gy == 0, 0.0, 1.0).astype(jnp.float32)
     high_weight = jnp.where(gy == count_y - 1, 0.0, 1.0).astype(jnp.float32)
 
-    first_x = x_halo(now_hbm, 0, now)
+    first_x = [x_halo(now_hbm, 0, now, comp) for comp in range(3)]
     asks = []
     for step in range(1, count_x):
         peer = lax.rem(gx + step, count_x)
         asks.append(send(request.at[peer], asked_x.at[gx], (peer, gy)))
     asked_x[gx] = request[gx]
     loads[0].wait()
-    edges(0, now)
-    first_y = y_halo(0)
+    first_y = []
+    for comp in range(3):
+        edges(0, now, comp)
+        first_y.append(y_halo(0, comp))
     for comp in range(3):
         for tile in range(disp_raw.shape[1]):
             disp_own[comp : comp + 1, tile * LANES : (tile + 1) * LANES] = disp_raw[comp, tile]
@@ -279,8 +279,9 @@
     def step_of(source, previous, target, shift):
         return lambda comp, index: wave_plane(comp, index, source, previous, factor, target, shift)
 
-    def fix(step, target, shift):
+    def fix(step, target, shift, comp):
         each_plane(
+            comp,
             [(0, planes)],
             lambda comp, index: y_corrections(
                 comp, index, y_got.at[step, 0], y_got.at[step, 1], low_weight, high_weight,
@@ -290,29 +291,31 @@
 
     inner, outer = [(2, planes - 2)], [(0, 2), (planes - 2, planes)]
     first = step_of(now, before, mid, 2)
-    each_plane(inner, first)
-    for copy in asks:
-        copy.wait()
-    for peer in range(count_y):
-        asked_t[peer] = asked_x[:, peer, :]
-    passes = []
-    for step in range(1, count_y):
-        peer = lax.rem(gy + step, count_y)
-        passes.append(send(asked_t.at[peer], asked_y.at[gy], (gx, peer)))
-    asked_y[gy] = asked_t[gy]
-    for copy in first_x:
-        copy.wait()
-    clear_outside(now)
-    each_plane(outer, first)
-    for copy in first_y:
-        copy.wait()
-    fix(0, mid, 2)
-
-    second_x = x_halo(mid, edge, mid)
-    edges(1, mid)
-    second_y = y_halo(1)
     second = step_of(mid, now, after, 0)
-    each_plane(inner, second)
+    for comp in range(3):
+        each_plane(comp, inner, first)
+    second_x, second_y, passes = [], [], []
+    for comp in range(3):
+        for copy in first_x[comp]:
+            copy.wait()
+        clear_outside(now, comp)
+        each_plane(comp, outer, first)
+        for copy in first_y[comp]:
+            copy.wait()
+        fix(0, mid, 2, comp)
+        second_x.append(x_halo(mid, edge, mid, comp))
+        edges(1, mid, comp)
+        second_y.append(y_halo(1, comp))
+        if comp == 0:
+            for copy in asks:
+                copy.wait()
+            for peer in range(count_y):
+                asked_t[peer] = asked_x[:, peer, :]
+            for step in range(1, count_y):
+                peer = lax.rem(gy + step, count_y)
+                passes.append(send(asked_t.at[peer], asked_y.at[gy], (gx, peer)))
+            asked_y[gy] = asked_t[gy]
+        each_plane(comp, inner, second)
     for copy in passes:
         copy.wait()
     cell = asked_y[...]
@@ -322,39 +325,49 @@
     )
     to_smem = pltpu.make_async_copy(rows_vmem, rows_smem, local_sems.at[6])
     to_smem.start()
-    for copy in second_x:
-        copy.wait()
-    clear_outside(mid)
-    each_plane(outer, second)
-    for copy in second_y:
-        copy.wait()
-    fix(1, after, 0)
-    store = pltpu.make_async_copy(after, after_hbm, local_sems.at[7])
-    store.start()
+    stores = []
+    for comp in range(3):
+        for copy in second_x[comp]:
+            copy.wait()
+        clear_outside(mid, comp)
+        each_plane(comp, outer, second)
+        for copy in second_y[comp]:
+            copy.wait()
+        fix(1, after, 0, comp)
+        store = pltpu.make_async_copy(after.at[comp], after_hbm.at[comp], store_sems.at[comp])
+        store.start()
+        stores.append(store)
     to_smem.wait()
 
     lane = lax.broadcasted_iota(jnp.int32, (1, LANES), 1)
     capacity = LANES // SLOTS
 
-    def find(source, carry):
-        for part in range(count_y):
-            held = jnp.zeros((1, LANES), jnp.float32)
-            for position in range(capacity):
-                place = rows_smem[part, source, position]
-                line = place >> 7
-                for comp in range(3):
-                    spot = position * SLOTS + comp
-                    values = after[comp, pl.ds(line, 1), :]
-                    shift = (spot - place) & (LANES - 1)
-                    held = jnp.where(lane == spot, pltpu.roll(values, shift, 1), held)
-            found[part, pl.ds(source, 1), :] = held
-        return carry
-
-    lax.fori_loop(0, count_x, find, 0)
+    unroll = 8
+
+    def find(part):
+        def run(chunk, carry):
+            for step in range(unroll):
+                source = chunk * unroll + step
+                held = jnp.zeros((1, LANES), jnp.float32)
+                for position in range(capacity):
+                    place = rows_smem[part, source, position]
+                    line = place >> 7
+                    for comp in range(3):
+                        spot = position * SLOTS + comp
+                        values = after[comp, pl.ds(line, 1), :]
+                        shift = (spot - place) & (LANES - 1)
+                        held = jnp.where(lane == spot, pltpu.roll(values, shift, 1), held)
+                found[part, pl.ds(source, 1), :] = held
+            return carry
+
+        lax.fori_loop(0, count_x // unroll, run, 0)
+
     answers = []
     for step in range(1, count_y):
         peer = lax.rem(gy + step, count_y)
+        find(peer)
         answers.append(send(found.at[peer], found_x.at[gy], (gx, peer)))
+    find(gy)
     found_x[gy] = found[gy]
     for copy in answers:
         copy.wait()
@@ -367,7 +380,8 @@
     reply_out[gx] = found_t[gx]
     for copy in finals + bulk + own:
         copy.wait()
-    store.wait()
+    for store in stores:
+        store.wait()
 
 
 def grid_steps(now, before, factor, request, disp, ids, params, live, count_x, count_y):
@@ -376,7 +390,7 @@
     hbm = pl.BlockSpec(memory_space=pl.ANY)
     vmem = pl.BlockSpec(memory_space=pltpu.VMEM)
     halo_rows = rows + 4 * PLANE
-    copies = 8 + 3 * (count_y - 1) + 2 * (count_x - 1) + 2 * (count_y - 1)
+    copies = 24 + 3 * (count_y - 1) + 2 * (count_x - 1) + 2 * (count_y - 1)
     planes = rows // PLANE
     stripes = ids.shape[1] // count_y
     return pl.pallas_call(
@@ -412,6 +426,7 @@
             pltpu.SemaphoreType.DMA((copies,)),
             pltpu.SemaphoreType.DMA((copies,)),
             pltpu.SemaphoreType.DMA((8,)),
+            pltpu.SemaphoreType.DMA((3,)),
         ],
         compiler_params=pltpu.CompilerParams(
             vmem_limit_bytes=VMEM_LIMIT, collective_id=1, has_side_effects=True
@@ -615,7 +630,9 @@
             terms = [block[corner * GROUP : corner * GROUP + GROUP] for corner in range(8)]
             while len(terms) > 1:
                 terms = [a + b for a, b in zip(terms[0::2], terms[1::2])]
-            out_ref[part, :, tile * LANES : (tile + 1) * LANES] = terms[0][0:3]
+            for comp in range(3):
+                line = comp * (own // LANES) + tile
+                out_ref[part, line : line + 1, :] = terms[0][comp : comp + 1]
         return carry
 
     lax.fori_loop(0, owners, fold, 0)
@@ -633,7 +650,7 @@
     return pl.pallas_call(
         box_kernel,
         out_shape=(
-            jax.ShapeDtypeStruct((owners, 3, own), f32),
+            jax.ShapeDtypeStruct((owners, 3 * own // LANES, LANES), f32),
             jax.ShapeDtypeStruct(field.shape, f32),
         ),
         in_specs=[smem, smem, hbm, vmem, vmem, vmem, hbm],
@@ -657,56 +674,75 @@
     )(layer_ids, slot_index, ids, disp, params, replies, field)
 
 
-def sum_kernel(parts_hbm, out_ref, got, send_sems, recv_sems, local_sem):
+def sum_kernel(
+    parts_hbm, out_ref, mine, near, sums, far, send_sems, recv_sems, local_sem
+):
     gx, gy = lax.axis_index("gx"), lax.axis_index("gy")
-    count = lax.axis_size("gy")
-    own = pltpu.make_async_copy(parts_hbm.at[gy], got.at[0], local_sem.at[0])
-    own.start()
+    pairs = lax.axis_size("gy") // 2
+    side, place = lax.rem(gy, 2), gy // 2
+    other = 2 * place + 1 - side
+    load = pltpu.make_async_copy(parts_hbm.at[:, side], mine, local_sem.at[0])
+    load.start()
     barrier = pltpu.get_barrier_semaphore()
-    for step in range(1, count):
-        peer = lax.rem(gy + step, count)
+    pl.semaphore_signal(barrier, inc=1, device_id=(gx, other), device_id_type=MESH)
+    for step in range(1, pairs):
+        peer = 2 * lax.rem(place + step, pairs) + side
         pl.semaphore_signal(barrier, inc=1, device_id=(gx, peer), device_id_type=MESH)
-    pl.semaphore_wait(barrier, count - 1)
+    pl.semaphore_wait(barrier, pairs)
+    swap = pltpu.make_async_remote_copy(
+        src_ref=parts_hbm.at[:, 1 - side],
+        dst_ref=near,
+        send_sem=send_sems.at[0],
+        recv_sem=recv_sems.at[0],
+        device_id=(gx, other),
+        device_id_type=MESH,
+    )
+    swap.start()
+    load.wait()
+    swap.wait()
     copies = []
-    for step in range(1, count):
-        peer = lax.rem(gy + step, count)
+    for step in range(1, pairs):
+        target = lax.rem(place + step, pairs)
+        sums[step] = mine[target] + near[target]
         copy = pltpu.make_async_remote_copy(
-            src_ref=parts_hbm.at[peer],
-            dst_ref=got.at[step],
+            src_ref=sums.at[step],
+            dst_ref=far.at[step],
             send_sem=send_sems.at[step],
             recv_sem=recv_sems.at[step],
-            device_id=(gx, peer),
+            device_id=(gx, 2 * target + side),
             device_id_type=MESH,
         )
         copy.start()
         copies.append(copy)
-    own.wait()
-    for copy in copies:
+    total = mine[place] + near[place]
+    for step, copy in enumerate(copies, 1):
         copy.wait()
-    terms = [got[step] for step in range(count)]
-    while len(terms) > 1:
-        terms = [a + b for a, b in zip(terms[0::2], terms[1::2])]
-    out_ref[...] = terms[0]
+        total = total + far[step]
+    out_ref[...] = total
 
 
 def sum_forces(parts):
-    count, comps, own = parts.shape
+    count, rows, _ = parts.shape
+    block = pltpu.VMEM((count // 2, rows, LANES), jnp.float32)
     return pl.pallas_call(
         sum_kernel,
-        out_shape=jax.ShapeDtypeStruct((comps, own), jnp.float32),
+        out_shape=jax.ShapeDtypeStruct((rows, LANES), jnp.float32),
         in_specs=[pl.BlockSpec(memory_space=pl.ANY)],
         out_specs=pl.BlockSpec(memory_space=pltpu.VMEM),
         scratch_shapes=[
-            pltpu.VMEM(parts.shape, jnp.float32),
-            pltpu.SemaphoreType.DMA((count,)),
-            pltpu.SemaphoreType.DMA((count,)),
+            block,
+            block,
+            block,
+            block,
+            pltpu.SemaphoreType.DMA((count // 2,)),
+            pltpu.SemaphoreType.DMA((count // 2,)),
             pltpu.SemaphoreType.DMA((1,)),
         ],
         compiler_params=pltpu.CompilerParams(
             vmem_limit_bytes=VMEM_LIMIT, collective_id=2, has_side_effects=True
         ),
         name="sum_forces",
-    )(parts)
+    )(parts.reshape(count // 2, 2, rows, LANES))
 
 
 def tiled_rows(field):
@@ -768,7 +804,7 @@
         replies.reshape(devices, LANES),
         after,
     )
-    summed = sum_forces(node_term)
+    summed = sum_forces(node_term).reshape(own_disp.shape)
     box_after = 2.0 * own_disp - box_before.reshape(3, -1) + STEP_SQUARE / node_mass * summed
     return (untiled_rows(after, grid_now.shape), box_after.reshape(box_now.shape))
 

time: 182 us -> 169 us (0.929)
  the two profiles are of different devices: /device:TPU:67 before, /device:TPU:98 now
where the time goes in v5:
time: 169 us
  Pallas kernels  166 us (98%)
  local copies, waits for them, and re-layouts  1.72 us (1%)
    pallas_call x1, Pallas kernels, box_forces(): pl.pallas_call(box_kernel, out_shape=(jax.ShapeDtypeStruct((owners, 3 * o...  108 us
    pallas_call x1, Pallas kernels, grid_steps(): pl.pallas_call(grid_kernel, out_shape=(jax.ShapeDtypeStruct(now.shape, f3...  43.7 us
    pallas_call x1, Pallas kernels, sum_forces(): pl.pallas_call(sum_kernel, out_shape=jax.ShapeDtypeStruct((rows, LANES),...  12.3 us

profile of v5, /device:TPU:98, one launch (start us, length us, event | category | flops | bytes accessed | tf_op | source)
XLA Modules:
  0.0 169.0 jit_solution(16782473933916118556)
XLA Ops:
  0.6 1.9 %rank_requests.1 = (s32[128,128]{1,0:T(8,128)}, s32[1,512]{1,0:T(1,128)}) custom-call(s32[1,512]{1,0:T(1,128)} %bitcast.42, s32[1,512]{1,0:T(1,128)} %cell_ref.1), custom_call_target="tpu_custom_call" | custom-call | tf_op jit(solution)/shard_map/rank_requests/pallas_call | solution.py:54
  3.2 43.7 %grid_steps.1 = (f32[3,2048,128]{2,1,0:T(8,128)}, f32[8,3,8960]{2,1,0:T(4,128)}, s32[8,72,128]{2,1,0:T(8,128)}, f32[8,24,128]{2,1,0:T(8,128)}, f32[16,8,128]{2,1,0:T(8,128)}) custom-call(f32[3,2048,128]{2,1,0:T(8,128)} %bitcast.30, f32[3,2048,128]{2,1,0:T(8,128)} %bitcast.31, f32[2048,128]{1,0:T(8,128)} %bitcast.32, s32[16,8,128]{2,1,0:T(8,128)} %bitcast.38, ...), custom_call_target="tpu_custom_call" | custom-call | tf_op jit(solution)/shard_map/grid_steps/pallas_call | solution.py:396
  46.9 0.0 copy-start.2
  46.9 0.0 copy-start
  46.9 0.0 copy-start.1
  46.9 107.8 %box_forces.1 = (f32[8,210,128]{2,1,0:T(8,128)}, f32[3,2048,128]{2,1,0:T(8,128)}) custom-call(s32[1,512]{1,0:T(1,128)} %layer_ref.1, s32[1,512]{1,0:T(1,128)} %get-tuple-element.11.slot_ref, s32[73728]{0:T(1024)} %bitcast.35, f32[8,3,8960]{2,1,0:T(4,128)} %get-tuple-element.14.disp_ref, f32[8,24,128]{2,1,0:T(8,128)} %get-tuple-element.15.params_ref, ...), custom_call_target="tpu_custom_call" | custom-call | tf_op jit(solution)/shard_map/box_forces/pallas_call | solution.py:650
  154.7 12.3 %sum_forces.1 = f32[210,128]{1,0:T(8,128)} custom-call(f32[4,2,210,128]{3,2,1,0:T(8,128)} %bitcast.33), custom_call_target="tpu_custom_call" | custom-call | tf_op jit(solution)/shard_map/sum_forces/pallas_call | solution.py:727
  167.1 0.9 reshape.116
  168.0 0.0 copy-done.2
  168.0 0.1 divide_reduce_fusion
  168.1 0.0 copy-done
  168.1 0.0 copy-done.1
  168.2 0.1 fusion
  168.3 0.8 copy.19
Async XLA Ops:
  46.9 121.1 %copy-start.2 = (f32[1,8960]{1,0:T(1,128)S(1)}, f32[1,8960]{1,0:T(1,128)}, u32[]{:S(2)}) copy-start(f32[1,8960]{1,0:T(1,128)} %param.21) | copy-start | bytes 107524
  46.9 121.2 %copy-start = (f32[3,1,8960]{2,1,0:T(1,128)S(1)}, f32[3,1,8960]{2,1,0:T(1,128)}, u32[]{:S(2)}) copy-start(f32[3,1,8960]{2,1,0:T(1,128)} %param.19) | copy-start | bytes 322564
  46.9 121.2 %copy-start.1 = (f32[3,1,8960]{2,1,0:T(1,128)S(1)}, f32[3,1,8960]{2,1,0:T(1,128)}, u32[]{:S(2)}) copy-start(f32[3,1,8960]{2,1,0:T(1,128)} %param.20) | copy-start | bytes 322564

commit v6 on v5

--- a/solution.py
+++ b/solution.py
@@ -15,7 +15,7 @@
 PLANE = 128
 VMEM_LIMIT = 58 * 2**20
 GATHER_UNROLL = 32
-SCATTER_UNROLL = 16
+SCATTER_UNROLL = 32
 LAYER_UNROLL = 16
 GROUP = 8
 MESH = pl.DeviceIdType.MESH
@@ -543,10 +543,10 @@
     total = table
     tiles = stripe // LANES
 
-    for part in range(owners):
+    def scatter_part(part, outer_carry):
         live = live_of(part)
 
-        def element(tile, carry, part=part, live=live):
+        def element(tile, carry):
             start = aligned(part * stripe + tile * LANES)
             grads = rows[pl.ds(start, LANES), 0:SLOTS].T
             slope = [[grads[3 * j + i : 3 * j + i + 1] for j in range(3)] for i in range(3)]
@@ -589,7 +589,7 @@
 
         lax.fori_loop(0, (live + LANES - 1) // LANES, element, 0)
 
-        def scatter(chunk, carry, part=part):
+        def scatter(chunk, carry):
             base = part * stripe + chunk * SCATTER_UNROLL
             for step in range(SCATTER_UNROLL):
                 line = rows[pl.ds(base + step, 1), :]
@@ -599,7 +599,9 @@
             return carry
 
         lax.fori_loop(0, (live + SCATTER_UNROLL - 1) // SCATTER_UNROLL, scatter, 0)
-
+        return outer_carry
+
+    lax.fori_loop(0, owners, scatter_part, 0)
     devices = reply_ref.shape[0]
     for position in range(LANES // SLOTS):
         values = reply_ref[...]

time: 169 us -> 160 us (0.947); the launches traced: 169 us -> 157 us
  Pallas kernels: 166 us -> 154 us
    pallas_call x1, Pallas kernels: 108 us -> 96.6 us  [box_forces(): pl.pallas_call(box_kernel, out_shape=(jax.ShapeDtypeStruct((owners, 3 * o...]
where the time goes in v6:
time: 160 us; the launch traced here: 157 us
  Pallas kernels  154 us (96%)
  local copies, waits for them, and re-layouts  1.72 us (1%)
    pallas_call x1, Pallas kernels, box_forces(): pl.pallas_call(box_kernel, out_shape=(jax.ShapeDtypeStruct((owners, 3 * o...  96.6 us
    pallas_call x1, Pallas kernels, grid_steps(): pl.pallas_call(grid_kernel, out_shape=(jax.ShapeDtypeStruct(now.shape, f3...  43.7 us
    pallas_call x1, Pallas kernels, sum_forces(): pl.pallas_call(sum_kernel, out_shape=jax.ShapeDtypeStruct((rows, LANES),...  11.8 us

profile of v6, /device:TPU:98, one launch (start us, length us, event | category | flops | bytes accessed | tf_op | source)
XLA Modules:
  0.0 157.3 jit_solution(125535594401753316)
XLA Ops:
  0.6 1.9 %rank_requests.1 = (s32[128,128]{1,0:T(8,128)}, s32[1,512]{1,0:T(1,128)}) custom-call(s32[1,512]{1,0:T(1,128)} %bitcast.42, s32[1,512]{1,0:T(1,128)} %cell_ref.1), custom_call_target="tpu_custom_call" | custom-call | tf_op jit(solution)/shard_map/rank_requests/pallas_call | solution.py:54
  3.2 43.7 %grid_steps.1 = (f32[3,2048,128]{2,1,0:T(8,128)}, f32[8,3,8960]{2,1,0:T(4,128)}, s32[8,72,128]{2,1,0:T(8,128)}, f32[8,24,128]{2,1,0:T(8,128)}, f32[16,8,128]{2,1,0:T(8,128)}) custom-call(f32[3,2048,128]{2,1,0:T(8,128)} %bitcast.30, f32[3,2048,128]{2,1,0:T(8,128)} %bitcast.31, f32[2048,128]{1,0:T(8,128)} %bitcast.32, s32[16,8,128]{2,1,0:T(8,128)} %bitcast.38, ...), custom_call_target="tpu_custom_call" | custom-call | tf_op jit(solution)/shard_map/grid_steps/pallas_call | solution.py:396
  46.9 0.0 copy-start.2
  46.9 0.0 copy-start
  46.9 0.0 copy-start.1
  46.9 96.6 %box_forces.1 = (f32[8,210,128]{2,1,0:T(8,128)}, f32[3,2048,128]{2,1,0:T(8,128)}) custom-call(s32[1,512]{1,0:T(1,128)} %layer_ref.1, s32[1,512]{1,0:T(1,128)} %get-tuple-element.11.slot_ref, s32[73728]{0:T(1024)} %bitcast.35, f32[8,3,8960]{2,1,0:T(4,128)} %get-tuple-element.14.disp_ref, f32[8,24,128]{2,1,0:T(8,128)} %get-tuple-element.15.params_ref, ...), custom_call_target="tpu_custom_call" | custom-call | tf_op jit(solution)/shard_map/box_forces/pallas_call | solution.py:652
  143.5 11.8 %sum_forces.1 = f32[210,128]{1,0:T(8,128)} custom-call(f32[4,2,210,128]{3,2,1,0:T(8,128)} %bitcast.33), custom_call_target="tpu_custom_call" | custom-call | tf_op jit(solution)/shard_map/sum_forces/pallas_call | solution.py:729
  155.3 0.9 reshape.116
  156.3 0.0 copy-done.2
  156.3 0.1 divide_reduce_fusion
  156.4 0.0 copy-done
  156.4 0.0 copy-done.1
  156.4 0.1 fusion
  156.5 0.8 copy.19
Async XLA Ops:
  46.9 109.4 %copy-start.2 = (f32[1,8960]{1,0:T(1,128)S(1)}, f32[1,8960]{1,0:T(1,128)}, u32[]{:S(2)}) copy-start(f32[1,8960]{1,0:T(1,128)} %param.21) | copy-start | bytes 107524
  46.9 109.5 %copy-start = (f32[3,1,8960]{2,1,0:T(1,128)S(1)}, f32[3,1,8960]{2,1,0:T(1,128)}, u32[]{:S(2)}) copy-start(f32[3,1,8960]{2,1,0:T(1,128)} %param.19) | copy-start | bytes 322564
  46.9 109.5 %copy-start.1 = (f32[3,1,8960]{2,1,0:T(1,128)S(1)}, f32[3,1,8960]{2,1,0:T(1,128)}, u32[]{:S(2)}) copy-start(f32[3,1,8960]{2,1,0:T(1,128)} %param.20) | copy-start | bytes 322564
